TPU v7x, 32 devices: a whole 2x2x4 slice. The times are simulated.
32 devices in a mesh: image: 4 (over y, core), space: 8 (over z, x).
Axes of the slice: x: 2, y: 2, z: 4, core: 2. Of those that a mesh axis runs over, the one named last changes fastest.
Arguments:
- positions: float32 [4, 3, 1024], P('image', None, 'space'), may hold values from -4 to 12
- velocity: float32 [4, 3, 1024], P('image', None, 'space'), may hold values from -3 to 3
- embed: bfloat16 [1024, 128], P('space'), may hold values from -6 to 6
- neighbours: int32 [1024, 32], P('space'), may hold values from 0 to 383
- send_up: int32 [1024], P('space'), may hold values from 0 to 127
- send_down: int32 [1024], P('space'), may hold values from 0 to 127
- climb: int32 [4], P('image'), may hold values from 0 to 1
- reset: int32 [4], P('image'), may hold values from 0 to 1
- filter_in: float32 [2, 16, 128], replicated, may hold values from -1.5 to 1.5
- filter_out: bfloat16 [2, 128, 128], replicated, may hold values from -0.5 to 0.5
- update_weight: bfloat16 [2, 128, 128], replicated, may hold values from -0.5 to 0.5
- readout: float32 [128], replicated, may hold values from -0.5 to 0.5
- spring: float32 [], replicated, may hold values from 2 to 20
- time_step: float32 [], replicated, may hold values from 0.05 to 0.2
- mixing: float32 [], replicated, may hold values from 0.05 to 0.3
Outputs:
- new_positions: float32 [4, 3, 1024], P('image', None, 'space')
- new_velocity: float32 [4, 3, 1024], P('image', None, 'space')
- energies: float32 [4], P('image')
All inputs are finite; a program needn't handle non-finite values.
Results may differ from a plain program's by a relative error of at most 0.0095.
Values may be sent and summed in bfloat16 or wider, within the bound.
A program may use at most 64 MiB of HBM per device.

v0:
```python
import jax
import jax.numpy as jnp
from jax import lax
from jax.sharding import PartitionSpec as P

EPSILON = 1e-06
BASIS_WIDTH = 0.6
BASIS_REACH = 6.0
HIGHEST = lax.Precision.HIGHEST


def with_halo(cells, sides, width, closed):
    for axis, dim in sides:
        count = lax.axis_size(axis)
        ends = count if closed else count - 1
        head = lax.slice_in_dim(cells, 0, width, axis=dim)
        tail = lax.slice_in_dim(cells, cells.shape[dim] - width, cells.shape[dim], axis=dim)
        cells = jnp.concatenate(
            [
                lax.ppermute(tail, axis, [(i, (i + 1) % count) for i in range(ends)]),
                cells,
                lax.ppermute(head, axis, [((i + 1) % count, i) for i in range(ends)]),
            ],
            axis=dim,
        )
    return cells


def silu_grad(values):
    sigmoid = jax.nn.sigmoid(values)
    return sigmoid * (1.0 + values * (1.0 - sigmoid))


def radial(sq_dist, basis_count):
    centres = lax.iota(jnp.float32, basis_count) * (BASIS_REACH / (basis_count - 1))
    scaled = (sq_dist[None, :] - centres[:, None]) / BASIS_WIDTH
    radial_vals = jnp.exp(-scaled * scaled)
    radial_slope = radial_vals * (-2.0 / BASIS_WIDTH) * scaled
    return (radial_vals, radial_slope)


def pair_filter(radial_vals, weight_in, weight_out):
    pre_act = lax.dot_general(
        radial_vals,
        weight_in,
        (((0,), (0,)), ((), ())),
        precision=HIGHEST,
        preferred_element_type=jnp.float32,
    )
    activated = jax.nn.silu(pre_act).astype(jnp.bfloat16)
    filter_vals = jnp.dot(activated, weight_out, preferred_element_type=jnp.float32)
    return (pre_act, filter_vals)


def gather_message(filter_vals, source_rows, per_atom):
    product = filter_vals * source_rows.astype(jnp.float32)
    return jnp.sum(product.reshape(-1, per_atom, product.shape[1]), axis=1)


def filter_back(grad_msg, source_rows, radial_vals, weight_in, weight_out, per_atom):
    pre_act, filter_vals = pair_filter(radial_vals, weight_in, weight_out)
    repeated = jnp.repeat(grad_msg, per_atom, axis=0)
    grad_filter = (repeated * source_rows.astype(jnp.float32)).astype(jnp.bfloat16)
    grad_source = filter_vals * repeated
    grad_act = lax.dot_general(
        grad_filter, weight_out, (((1,), (1,)), ((), ())), preferred_element_type=jnp.float32
    )
    grad_pre = grad_act * silu_grad(pre_act)
    grad_radial = lax.dot_general(
        weight_in,
        grad_pre,
        (((1,), (1,)), ((), ())),
        precision=HIGHEST,
        preferred_element_type=jnp.float32,
    )
    return (grad_source, grad_radial)


def exchange_coords(to_lower, to_upper):
    stacked = jnp.stack([to_lower, to_upper])
    extended = with_halo(stacked, (("space", 0),), 1, True)
    return (extended[0], extended[3])


def exchange_rows(to_lower, to_upper):
    stacked = jnp.stack([to_lower, to_upper])
    extended = with_halo(stacked, (("space", 0),), 1, True)
    return (extended[0], extended[3])


def exchange_grads(to_lower, to_upper):
    stacked = jnp.stack([to_lower, to_upper])
    extended = with_halo(stacked.astype(jnp.bfloat16), (("space", 0),), 1, True).astype(
        stacked.dtype
    )
    return (extended[0], extended[3])


def per_device(
    positions,
    velocity,
    embed,
    neighbours,
    send_up,
    send_down,
    climb,
    reset,
    filter_in,
    filter_out,
    update_weight,
    readout,
    spring,
    time_step,
    mixing,
):
    domain = lax.axis_index("space")
    domains = lax.axis_size("space")
    coords = positions[0]
    speed_now = velocity[0]
    atom_rows = coords.shape[1]
    per_atom = neighbours.shape[1]
    ghost_rows = send_up.shape[0]
    channels = embed.shape[1]
    first_axis = (lax.iota(jnp.int32, 3) == 0).astype(jnp.float32)[:, None]
    low_flat, high_flat = exchange_coords(
        coords[:, send_down].reshape(-1), coords[:, send_up].reshape(-1)
    )
    low_embed, high_embed = exchange_rows(embed[send_down].reshape(-1), embed[send_up].reshape(-1))
    low_shift = jnp.where(domain == 0, -domains, 0).astype(jnp.float32)
    high_shift = jnp.where(domain == domains - 1, domains, 0).astype(jnp.float32)
    low_pos = low_flat.reshape(3, ghost_rows) + first_axis * low_shift
    high_pos = high_flat.reshape(3, ghost_rows) + first_axis * high_shift
    ext_coords = jnp.concatenate([coords, low_pos, high_pos], axis=1)
    ghost_embed = jnp.concatenate(
        [low_embed.reshape(ghost_rows, channels), high_embed.reshape(ghost_rows, channels)], axis=0
    )
    ext_embed = jnp.concatenate([embed, ghost_embed], axis=0)
    slot_ids = neighbours.reshape(-1)
    pair_vec = ext_coords[:, slot_ids] - jnp.repeat(coords, per_atom, axis=1)
    sq_dist = jnp.sum(pair_vec * pair_vec, axis=0)
    radial_vals, radial_slope = radial(sq_dist, filter_in.shape[1])
    embed_rows = ext_embed[slot_ids]
    pre_one, filter_one = pair_filter(radial_vals, filter_in[0], filter_out[0])
    message_one = gather_message(filter_one, embed_rows, per_atom).astype(jnp.bfloat16)
    update_one = jnp.dot(message_one, update_weight[0], preferred_element_type=jnp.float32)
    hidden = (embed.astype(jnp.float32) + jax.nn.silu(update_one)).astype(jnp.bfloat16)
    low_hidden, high_hidden = exchange_rows(
        hidden[send_down].reshape(-1), hidden[send_up].reshape(-1)
    )
    ghost_hidden = jnp.concatenate(
        [low_hidden.reshape(ghost_rows, channels), high_hidden.reshape(ghost_rows, channels)],
        axis=0,
    )
    ext_hidden = jnp.concatenate([hidden, ghost_hidden], axis=0)
    hidden_rows = ext_hidden[slot_ids]
    pre_two, filter_two = pair_filter(radial_vals, filter_in[1], filter_out[1])
    message_two = gather_message(filter_two, hidden_rows, per_atom).astype(jnp.bfloat16)
    update_two = jnp.dot(message_two, update_weight[1], preferred_element_type=jnp.float32)
    energy_part = jnp.sum(jnp.dot(jax.nn.silu(update_two), readout, precision=HIGHEST))
    grad_update_two = (silu_grad(update_two) * readout[None, :]).astype(jnp.bfloat16)
    grad_msg_two = lax.dot_general(
        grad_update_two,
        update_weight[1],
        (((1,), (1,)), ((), ())),
        preferred_element_type=jnp.float32,
    )
    grad_source_two, grad_radial_two = filter_back(
        grad_msg_two, hidden_rows, radial_vals, filter_in[1], filter_out[1], per_atom
    )
    grad_hidden = (
        jnp.zeros((atom_rows + 2 * ghost_rows, channels), jnp.float32)
        .at[slot_ids]
        .add(grad_source_two)
    )
    back_lower, back_upper = exchange_grads(
        grad_hidden[atom_rows : atom_rows + ghost_rows].reshape(-1),
        grad_hidden[atom_rows + ghost_rows :].reshape(-1),
    )
    grad_local = grad_hidden[:atom_rows].at[send_down].add(back_lower.reshape(ghost_rows, channels))
    grad_local = grad_local.at[send_up].add(back_upper.reshape(ghost_rows, channels))
    grad_update_one = (grad_local * silu_grad(update_one)).astype(jnp.bfloat16)
    grad_msg_one = lax.dot_general(
        grad_update_one,
        update_weight[0],
        (((1,), (1,)), ((), ())),
        preferred_element_type=jnp.float32,
    )
    grad_source_one, grad_radial_one = filter_back(
        grad_msg_one, embed_rows, radial_vals, filter_in[0], filter_out[0], per_atom
    )
    grad_sq = jnp.sum((grad_radial_one + grad_radial_two) * radial_slope, axis=0)
    pair_grad = 2.0 * grad_sq[None, :] * pair_vec
    ext_grad = (
        jnp.zeros((3, atom_rows + 2 * ghost_rows), jnp.float32).at[:, slot_ids].add(pair_grad)
    )
    return_lower, return_upper = exchange_grads(
        ext_grad[:, atom_rows : atom_rows + ghost_rows].reshape(-1),
        ext_grad[:, atom_rows + ghost_rows :].reshape(-1),
    )
    gradient = ext_grad[:, :atom_rows] - jnp.sum(pair_grad.reshape(3, atom_rows, per_atom), axis=2)
    gradient = gradient.at[:, send_down].add(return_lower.reshape(3, ghost_rows))
    gradient = gradient.at[:, send_up].add(return_upper.reshape(3, ghost_rows))
    forces = -gradient
    band_rows = with_halo(positions, (("image", 0),), 1, False)
    ahead_vec = band_rows[2] - coords
    behind = coords - band_rows[0]
    image_index = lax.axis_index("image")
    images = lax.axis_size("image")
    movable = (image_index > 0) & (image_index < images - 1)
    climbing = climb[0] > 0
    energy, ahead_sq, behind_sq = lax.psum(
        (energy_part, jnp.sum(ahead_vec * ahead_vec), jnp.sum(behind * behind)), "space"
    )
    ahead_norm = jnp.sqrt(ahead_sq + EPSILON)
    behind_norm = jnp.sqrt(behind_sq + EPSILON)
    tangent = ahead_vec / ahead_norm + behind / behind_norm
    tangent_sq = lax.psum(jnp.sum(tangent * tangent), "space")
    unit_tangent = tangent / jnp.sqrt(tangent_sq + EPSILON)
    parallel = lax.psum(jnp.sum(forces * unit_tangent), "space")
    spring_part = spring * (ahead_norm - behind_norm)
    band_force = jnp.where(
        climbing,
        forces - 2.0 * parallel * unit_tangent,
        forces - parallel * unit_tangent + spring_part * unit_tangent,
    )
    band_force = jnp.where(movable, band_force, 0.0)
    force_total, speed_total = lax.psum(
        (jnp.sum(band_force * band_force), jnp.where(movable, jnp.sum(speed_now * speed_now), 0.0)),
        ("image", "space"),
    )
    force_norm = jnp.sqrt(force_total + EPSILON)
    speed_norm = jnp.sqrt(speed_total + EPSILON)
    mixed = (1.0 - mixing) * speed_now + mixing * (speed_norm / force_norm) * band_force
    kept_speed = jnp.where(reset[0] > 0, 0.0, mixed)
    new_speed = jnp.where(movable, kept_speed + time_step * band_force, 0.0)
    new_coords = coords + time_step * new_speed
    return (new_coords[None], new_speed[None], energy.reshape(1))


def solution(mesh):
    placed = (
        P("image", None, "space"),
        P("image", None, "space"),
        P("space", None),
        P("space", None),
        P("space"),
        P("space"),
        P("image"),
        P("image"),
        P(),
        P(),
        P(),
        P(),
        P(),
        P(),
        P(),
    )
    return jax.shard_map(
        per_device,
        mesh=mesh,
        in_specs=placed,
        out_specs=(P("image", None, "space"), P("image", None, "space"), P("image")),
        check_vma=False,
    )
```

profile of v0, /device:TPU:0, one launch (start us, length us, event | category | flops | bytes accessed | tf_op | source)
XLA Modules:
  0.0 277.9 jit_solution(17622944651902055232)
XLA Ops:
  2.6 3.0 %collective-permute-start.11 = (f32[1,3,128]{2,1,0:T(4,128)S(1)}, f32[1,3,128]{2,1,0:T(4,128)S(1)}, u32[]{:S(2)}, u32[]{:S(2)}) collective-permute-start(f32[1,3,128]{2,1,0:T(4,128)S(1)} %copy.135), channel_id=1, source_target_pairs={{0,8},{8,16},{16,24},{1,9},{9,17},{17,25},{2,10},{10,18},{18,26},{... | collective-permute-start | bytes 4616 | tf_op jit(solution)/shard_map/ppermute | solution.py:20
  7.1 6.0 %collective-permute-start.1 = (f32[1,384]{1,0:T(1,128)S(1)}, f32[1,384]{1,0:T(1,128)S(1)}, u32[]{:S(2)}, u32[]{:S(2)}) collective-permute-start(f32[1,384]{1,0:T(1,128)S(1)} %bitcast.234), channel_id=1, source_target_pairs={{1,0},{2,1},{3,2},{4,3},{5,4},{6,5},{7,6},{0,7},{9,8},{10,9},{11,1... | collective-permute-start | bytes 4616 | tf_op jit(solution)/shard_map/ppermute | solution.py:22
  23.8 4.8 %collective-permute-start.3 = (bf16[1,16384]{1,0:T(2,128)(2,1)S(1)}, bf16[1,16384]{1,0:T(2,128)(2,1)S(1)}, u32[]{:S(2)}, u32[]{:S(2)}) collective-permute-start(bf16[1,16384]{1,0:T(2,128)(2,1)S(1)} %bitcast.216), channel_id=1, source_target_pairs={{1,0},{2,1},{3,2},{4,3},{5,4},{6,5},{7,6},{0,7},{9,8},{10,9},{11,1... | collective-permute-start | bytes 98312 | tf_op jit(solution)/shard_map/ppermute | solution.py:22
  28.9 10.8 %gather_fusion.2 = f32[4096,3]{1,0:T(8,128)S(1)} fusion(f32[3,384]{0,1:T(8,128)S(1)} %copy.75, s32[4096]{0:T(1024)S(1)} %broadcast_clamp_fusion), kind=kCustom, calls=%fused_computation.2 | custom fusion | bytes 114688 | tf_op jit(solution)/shard_map/gather | solution.py:139
  39.7 1.8 bitcast_subtract_fusion
  41.5 4.8 %fusion.11 = f32[4096,128]{1,0:T(8,128)} fusion(f32[16]{0:T(128)S(1)} %iota_multiply_fusion, f32[4096]{0:T(1024)S(1)} %get-tuple-element.33, f32[2,16,128]{2,1,0:T(8,128)S(1)} %copy-done.5), kind=kOutput, calls=%fused_computation.46 | convolution fusion | flops 100925440 | bytes 2122240 | tf_op jit(solution)/shard_map/dot_general | solution.py:43
  46.3 4.8 %fusion.13 = f32[4096,128]{1,0:T(8,128)} fusion(f32[16]{0:T(128)S(1)} %iota_multiply_fusion, f32[4096]{0:T(1024)S(1)} %get-tuple-element.33, f32[2,16,128]{2,1,0:T(8,128)S(1)} %copy-done.5), kind=kOutput, calls=%fused_computation.47 | convolution fusion | flops 100925440 | bytes 2122240 | tf_op jit(solution)/shard_map/dot_general | solution.py:43
  51.8 19.7 %all-reduce.2 = (f32[]{:T(128)}, f32[]{:T(128)}) all-reduce(f32[]{:T(128)} %get-tuple-element.21, f32[]{:T(128)} %get-tuple-element.20), channel_id=1, replica_groups=mesh['image'=4,'space'=8] {'space'}, use_global_device_ids=true, to_apply=%region_14.15 | all-reduce | flops 2 | bytes 16 | tf_op jit(solution)/shard_map/psum | solution.py:211
  73.3 12.1 %gather_fusion.5 = bf16[4096,128]{1,0:T(8,128)(2,1)S(1)} fusion(bf16[384,128]{1,0:T(8,128)(2,1)S(1)} %pad_maximum_fusion, s32[4096]{0:T(1024)S(1)} %broadcast_clamp_fusion), kind=kCustom, calls=%fused_computation.5 | custom fusion | bytes 2113536 | tf_op jit(solution)/shard_map/gather | solution.py:142
  85.4 2.4 bitcast_reduce_fusion.1
  90.8 4.7 %collective-permute-start.5 = (bf16[1,16384]{1,0:T(2,128)(2,1)}, bf16[1,16384]{1,0:T(2,128)(2,1)S(1)}, u32[]{:S(2)}, u32[]{:S(2)}) collective-permute-start(bf16[1,16384]{1,0:T(2,128)(2,1)} %bitcast.186), channel_id=1, source_target_pairs={{1,0},{2,1},{3,2},{4,3},{5,4},{6,5},{7,6},{0,7},{9,8},{10,9},{11,1... | collective-permute-start | bytes 98312 | tf_op jit(solution)/shard_map/ppermute | solution.py:22
  96.1 17.9 %psum.52 = f32[]{:T(128)} all-reduce(f32[]{:T(128)} %get-tuple-element.30), channel_id=1, replica_groups=mesh['image'=4,'space'=8] {'space'}, use_global_device_ids=true, to_apply=%region_18.19 | all-reduce | flops 1 | bytes 8 | tf_op jit(solution)/shard_map/psum | solution.py:217
  116.0 14.9 %gather_fusion.8 = bf16[4096,128]{1,0:T(8,128)(2,1)} fusion(bf16[384,128]{1,0:T(8,128)(2,1)S(1)} %pad_maximum_fusion.1, s32[4096]{0:T(1024)S(1)} %broadcast_clamp_fusion), kind=kCustom, calls=%fused_computation.8 | custom fusion | bytes 2113536 | tf_op jit(solution)/shard_map/gather | solution.py:155
  130.9 2.7 bitcast_reduce_fusion
  135.3 2.2 convolution_multiply_fusion
  139.0 22.7 %scatter_custom_fusion = f32[384,128]{1,0:T(8,128)S(1)} fusion(s32[4096]{0:T(1024)S(1)} %bitcast.219, f32[4096,128]{1,0:T(8,128)} %bitcast_multiply_fusion, f32[]{:T(128)} %constant.21.clone.1), kind=kCustom, calls=%fused_computation.56 | custom fusion | flops 524288 | bytes 197120 | tf_op jit(solution)/shard_map/scatter-add | solution.py:173
  161.8 2.0 collective-permute-start.6
  163.9 2.8 %collective-permute-start.7 = (bf16[1,16384]{1,0:T(2,128)(2,1)S(1)}, bf16[1,16384]{1,0:T(2,128)(2,1)S(1)}, u32[]{:S(2)}, u32[]{:S(2)}) collective-permute-start(bf16[1,16384]{1,0:T(2,128)(2,1)S(1)} %bitcast.203), channel_id=1, source_target_pairs={{1,0},{2,1},{3,2},{4,3},{5,4},{6,5},{7,6},{0,7},{9,8},{10,9},{11,1... | collective-permute-start | bytes 98312 | tf_op jit(solution)/shard_map/ppermute | solution.py:22
  175.0 1.9 fusion.50
  176.8 1.9 fusion.5
  178.8 24.8 %scatter_custom_fusion.3 = f32[3,384]{0,1:T(8,128)S(1)} fusion(s32[4096]{0:T(1024)S(1)} %bitcast.220, f32[3,4096]{0,1:T(8,128)} %get-tuple-element.32, f32[4096]{0:T(1024)S(1)} %broadcast_multiply_fusion, f32[]{:T(128)} %constant.21.clone.1), kind=kCustom, calls=%fused_computation.21 | custom fusion | flops 24576 | bytes 70148 | tf_op jit(solution)/shard_map/scatter-add | solution.py:194
  204.1 4.6 %collective-permute-start.9 = (bf16[1,384]{1,0:T(2,128)(2,1)S(1)}, bf16[1,384]{1,0:T(2,128)(2,1)S(1)}, u32[]{:S(2)}, u32[]{:S(2)}) collective-permute-start(bf16[1,384]{1,0:T(2,128)(2,1)S(1)} %bitcast.229), channel_id=1, source_target_pairs={{1,0},{2,1},{3,2},{4,3},{5,4},{6,5},{7,6},{0,7},{9,8},{10,9},{11,1... | collective-permute-start | bytes 2312 | tf_op jit(solution)/shard_map/ppermute | solution.py:22
  213.7 22.6 %all-reduce.1 = (f32[]{:T(128)}, f32[1]{0:T(128)}) all-reduce(f32[]{:T(128)} %multiply_reduce_fusion.3, f32[1]{0:T(128)} %bitcast.34), channel_id=1, replica_groups=mesh['image'=4,'space'=8] {'space'}, use_global_device_ids=true, to_apply=%region_20.21 | all-reduce | flops 2 | bytes 16 | tf_op jit(solution)/shard_map/psum | solution.py:219
  238.2 37.1 %all-reduce = (f32[]{:T(128)}, f32[]{:T(128)}) all-reduce(f32[]{:T(128)S(6)} %select_n.69, f32[]{:T(128)} %get-tuple-element.28), channel_id=1, replica_groups=mesh['image'=4,'space'=8] {'image','space'}, use_global_device_ids=true, to_apply=%region_1.2 | all-reduce | flops 2 | bytes 16 | tf_op jit(solution)/shard_map/psum | solution.py:227
  (125 shorter events, 35.6 us)
Async XLA Ops:
  1.3 49.8 %collective-permute-start.10 = (f32[1,3,128]{2,1,0:T(4,128)S(1)}, f32[1,3,128]{2,1,0:T(4,128)S(1)}, u32[]{:S(2)}, u32[]{:S(2)}) collective-permute-start(f32[1,3,128]{2,1,0:T(4,128)S(1)} %copy.135), channel_id=1, source_target_pairs={{8,0},{16,8},{24,16},{9,1},{17,9},{25,17},{10,2},{18,10},{26,18},{... | collective-permute-start | bytes 4616 | tf_op jit(solution)/shard_map/ppermute | solution.py:22
  2.6 48.5 %collective-permute-start.11 = (f32[1,3,128]{2,1,0:T(4,128)S(1)}, f32[1,3,128]{2,1,0:T(4,128)S(1)}, u32[]{:S(2)}, u32[]{:S(2)}) collective-permute-start(f32[1,3,128]{2,1,0:T(4,128)S(1)} %copy.135), channel_id=1, source_target_pairs={{0,8},{8,16},{16,24},{1,9},{9,17},{17,25},{2,10},{10,18},{18,26},{... | collective-permute-start | bytes 4616 | tf_op jit(solution)/shard_map/ppermute | solution.py:20
  7.1 16.6 %collective-permute-start.1 = (f32[1,384]{1,0:T(1,128)S(1)}, f32[1,384]{1,0:T(1,128)S(1)}, u32[]{:S(2)}, u32[]{:S(2)}) collective-permute-start(f32[1,384]{1,0:T(1,128)S(1)} %bitcast.234), channel_id=1, source_target_pairs={{1,0},{2,1},{3,2},{4,3},{5,4},{6,5},{7,6},{0,7},{9,8},{10,9},{11,1... | collective-permute-start | bytes 4616 | tf_op jit(solution)/shard_map/ppermute | solution.py:22
  14.5 14.1 %collective-permute-start = (f32[1,384]{1,0:T(1,128)S(1)}, f32[1,384]{1,0:T(1,128)S(1)}, u32[]{:S(2)}, u32[]{:S(2)}) collective-permute-start(f32[1,384]{1,0:T(1,128)S(1)} %bitcast.233), channel_id=1, source_target_pairs={{0,1},{1,2},{2,3},{3,4},{4,5},{5,6},{6,7},{7,0},{8,9},{9,10},{10,1... | collective-permute-start | bytes 4616 | tf_op jit(solution)/shard_map/ppermute | solution.py:20
  16.0 56.9 %collective-permute-start.2 = (bf16[1,16384]{1,0:T(2,128)(2,1)S(1)}, bf16[1,16384]{1,0:T(2,128)(2,1)S(1)}, u32[]{:S(2)}, u32[]{:S(2)}) collective-permute-start(bf16[1,16384]{1,0:T(2,128)(2,1)S(1)} %bitcast.215), channel_id=1, source_target_pairs={{0,1},{1,2},{2,3},{3,4},{4,5},{5,6},{6,7},{7,0},{8,9},{9,10},{10,1... | collective-permute-start | bytes 98312 | tf_op jit(solution)/shard_map/ppermute | solution.py:20
  23.8 49.3 %collective-permute-start.3 = (bf16[1,16384]{1,0:T(2,128)(2,1)S(1)}, bf16[1,16384]{1,0:T(2,128)(2,1)S(1)}, u32[]{:S(2)}, u32[]{:S(2)}) collective-permute-start(bf16[1,16384]{1,0:T(2,128)(2,1)S(1)} %bitcast.216), channel_id=1, source_target_pairs={{1,0},{2,1},{3,2},{4,3},{5,4},{6,5},{7,6},{0,7},{9,8},{10,9},{11,1... | collective-permute-start | bytes 98312 | tf_op jit(solution)/shard_map/ppermute | solution.py:22
  39.6 1.8 copy-start.5
  41.5 9.7 %copy-start.7 = (f32[1,3,128]{2,0,1:T(1,128)S(1)}, f32[1,3,128]{2,0,1:T(1,128)}, u32[]{:S(2)}) copy-start(f32[1,3,128]{2,0,1:T(1,128)} %param.15) | copy-start | bytes 4612
  41.5 31.8 %copy-start = (bf16[128,128]{1,0:T(8,128)(2,1)S(1)}, bf16[128,128]{1,0:T(8,128)(2,1)}, u32[]{:S(2)}) copy-start(bf16[128,128]{1,0:T(8,128)(2,1)} %param.17) | copy-start | bytes 98308
  85.4 2.4 copy-start.8
  90.1 24.7 %collective-permute-start.4 = (bf16[1,16384]{1,0:T(2,128)(2,1)S(1)}, bf16[1,16384]{1,0:T(2,128)(2,1)}, u32[]{:S(2)}, u32[]{:S(2)}) collective-permute-start(bf16[1,16384]{1,0:T(2,128)(2,1)S(1)} %bitcast.217), channel_id=1, source_target_pairs={{0,1},{1,2},{2,3},{3,4},{4,5},{5,6},{6,7},{7,0},{8,9},{9,10},{10,1... | collective-permute-start | bytes 98312 | tf_op jit(solution)/shard_map/ppermute | solution.py:20
  90.8 25.0 %collective-permute-start.5 = (bf16[1,16384]{1,0:T(2,128)(2,1)}, bf16[1,16384]{1,0:T(2,128)(2,1)S(1)}, u32[]{:S(2)}, u32[]{:S(2)}) collective-permute-start(bf16[1,16384]{1,0:T(2,128)(2,1)} %bitcast.186), channel_id=1, source_target_pairs={{1,0},{2,1},{3,2},{4,3},{5,4},{6,5},{7,6},{0,7},{9,8},{10,9},{11,1... | collective-permute-start | bytes 98312 | tf_op jit(solution)/shard_map/ppermute | solution.py:22
  116.0 14.9 %copy-start.11 = (bf16[2,128,128]{2,1,0:T(8,128)(2,1)S(1)}, bf16[2,128,128]{2,1,0:T(8,128)(2,1)}, u32[]{:S(2)}) copy-start(bf16[2,128,128]{2,1,0:T(8,128)(2,1)} %param.24) | copy-start | bytes 196612
  130.9 2.8 copy-start.9
  130.9 2.9 %copy-start.13 = (f32[128]{0:T(128)S(1)}, f32[128]{0:T(128)}, u32[]{:S(2)}) copy-start(f32[128]{0:T(128)} %param.26) | copy-start | bytes 1540
  130.9 3.1 %copy-start.1 = (bf16[4096,128]{1,0:T(8,128)(2,1)S(1)}, bf16[4096,128]{1,0:T(8,128)(2,1)}, u32[]{:S(2)}) copy-start(bf16[4096,128]{1,0:T(8,128)(2,1)} %gather_fusion.8) | copy-start | bytes 3145732
  133.8 3.7 %copy-start.6 = (f32[128,128]{1,0:T(8,128)}, f32[128,128]{1,0:T(8,128)S(1)}, u32[]{:S(2)}) copy-start(f32[128,128]{1,0:T(8,128)S(1)} %fusion.28) | copy-start | bytes 196612
  161.8 7.1 %collective-permute-start.6 = (bf16[1,16384]{1,0:T(2,128)(2,1)S(1)}, bf16[1,16384]{1,0:T(2,128)(2,1)S(1)}, u32[]{:S(2)}, u32[]{:S(2)}) collective-permute-start(bf16[1,16384]{1,0:T(2,128)(2,1)S(1)} %bitcast.201), channel_id=1, source_target_pairs={{0,1},{1,2},{2,3},{3,4},{4,5},{5,6},{6,7},{7,0},{8,9},{9,10},{10,1... | collective-permute-start | bytes 98312 | tf_op jit(solution)/shard_map/ppermute | solution.py:20
  163.9 5.0 %collective-permute-start.7 = (bf16[1,16384]{1,0:T(2,128)(2,1)S(1)}, bf16[1,16384]{1,0:T(2,128)(2,1)S(1)}, u32[]{:S(2)}, u32[]{:S(2)}) collective-permute-start(bf16[1,16384]{1,0:T(2,128)(2,1)S(1)} %bitcast.203), channel_id=1, source_target_pairs={{1,0},{2,1},{3,2},{4,3},{5,4},{6,5},{7,6},{0,7},{9,8},{10,9},{11,1... | collective-permute-start | bytes 98312 | tf_op jit(solution)/shard_map/ppermute | solution.py:22
  170.9 2.9 %copy-start.12 = (bf16[2,128,128]{2,1,0:T(8,128)(2,1)S(1)}, bf16[2,128,128]{2,1,0:T(8,128)(2,1)}, u32[]{:S(2)}) copy-start(bf16[2,128,128]{2,1,0:T(8,128)(2,1)} %param.24) | copy-start | bytes 196612
  175.0 1.9 copy-start.4
  203.7 73.1 %copy-start.10 = (f32[1,3,128]{2,0,1:T(1,128)S(1)}, f32[1,3,128]{2,0,1:T(1,128)}, u32[]{:S(2)}) copy-start(f32[1,3,128]{2,0,1:T(1,128)} %param.16) | copy-start | bytes 4612
  203.8 6.3 %collective-permute-start.8 = (bf16[1,384]{1,0:T(2,128)(2,1)S(1)}, bf16[1,384]{1,0:T(2,128)(2,1)S(1)}, u32[]{:S(2)}, u32[]{:S(2)}) collective-permute-start(bf16[1,384]{1,0:T(2,128)(2,1)S(1)} %bitcast.227), channel_id=1, source_target_pairs={{0,1},{1,2},{2,3},{3,4},{4,5},{5,6},{6,7},{7,0},{8,9},{9,10},{10,1... | collective-permute-start | bytes 2312 | tf_op jit(solution)/shard_map/ppermute | solution.py:20
  204.1 6.0 %collective-permute-start.9 = (bf16[1,384]{1,0:T(2,128)(2,1)S(1)}, bf16[1,384]{1,0:T(2,128)(2,1)S(1)}, u32[]{:S(2)}, u32[]{:S(2)}) collective-permute-start(bf16[1,384]{1,0:T(2,128)(2,1)S(1)} %bitcast.229), channel_id=1, source_target_pairs={{1,0},{2,1},{3,2},{4,3},{5,4},{6,5},{7,6},{0,7},{9,8},{10,9},{11,1... | collective-permute-start | bytes 2312 | tf_op jit(solution)/shard_map/ppermute | solution.py:22
  (2 other events, 3.3 us)
where the time goes:
time: 280 us; the launch traced here: 278 us
  blocking collectives  97.3 us (35%)
  other arithmetic  65.8 us (24%)
  local copies, waits for them, and re-layouts  49.3 us (18%)
  starting transfers between devices  29.6 us (11%)
  matrix products  25.5 us (9%)
  between operations  9.17 us (3%)
    psum x1, blocking collectives, per_device(): lax.psum((jnp.sum(band_force * band_force), jnp.where(movable, jnp.sum(sp...  37.1 us
    scatter-add x1, other arithmetic, per_device(): jnp.zeros((3, atom_rows + 2 * ghost_rows), jnp.float32).at[:, slot_ids]  24.8 us
    ppermute x6, starting transfers between devices, with_halo(): lax.ppermute(head, axis, [((i + 1) % count, i) for i in range(ends)])  24.1 us
    scatter-add x1, other arithmetic, per_device(): grad_hidden = jnp.zeros((atom_rows + 2 * ghost_rows, channels), jnp.float...  22.7 us
    psum x1, blocking collectives, per_device(): parallel = lax.psum(jnp.sum(forces * unit_tangent), 'space')  22.6 us
    psum x1, blocking collectives, per_device(): lax.psum((energy_part, jnp.sum(ahead_vec * ahead_vec), jnp.sum(behind * b...  19.7 us
    psum x1, blocking collectives, per_device(): tangent_sq = lax.psum(jnp.sum(tangent * tangent), 'space')  17.9 us
    gather x1, local copies, waits for them, and re-layouts, per_device(): hidden_rows = ext_hidden[slot_ids]  14.9 us
  transfers between devices with their start and end apart: 12, of which 2 were waited for; matrix products, arithmetic and copies ran while one was open for 13% of the time, Pallas kernels for 0%

commit v1 on v0

v1 whole, which is shorter than its diff:
```python
import functools
import jax
import jax.numpy as jnp
from jax import lax
from jax.experimental import pallas as pl
from jax.experimental.pallas import tpu as pltpu
from jax.sharding import PartitionSpec as P

EPSILON = 1e-06
BASIS_WIDTH = 0.6
BASIS_REACH = 6.0
F32 = jnp.float32
BF16 = jnp.bfloat16
MESH = pl.DeviceIdType.MESH


def dot(left, right):
    return jnp.dot(left, right, preferred_element_type=F32)


def dot_nt(left, right):
    return lax.dot_general(left, right, (((1,), (1,)), ((), ())), preferred_element_type=F32)


def dot_tn(left, right):
    return lax.dot_general(left, right, (((0,), (0,)), ((), ())), preferred_element_type=F32)


def gate(values):
    return 0.5 * jnp.tanh(0.5 * values) + 0.5


def split_two(values):
    high = values.astype(BF16)
    low = (values - high.astype(F32)).astype(BF16)
    return high, low


def onehot(mask):
    return jnp.where(mask, 1.0, 0.0).astype(BF16)


def body(
    n_space, n_image,
    pos_ref, vel_ref, emb_ref, nb_ref, up_ref, down_ref, climb_ref, reset_ref,
    fin_ref, fout_ref, uw_ref, read_ref, spring_ref, step_ref, mix_ref,
    newpos_ref, newvel_ref, energy_ref,
    pos8, prev8, next8, coord, coord_src, ext_emb, emb_src, ext_hid, hid_src,
    grad_all, grad_src, grad_in, force_src, force_in,
    sel, sel_t, oh, oht, nb_t, pv_all, slope_all, pre_two, ds_one, ds_two,
    rows_one, rows_two, filt_two, drad, w_in, w_back,
    norm_src, norm_in, sum_src, sum_in, band_src, band_in,
    send, recv, norm_send, norm_recv, sum_send, sum_recv, band_send, band_recv,
):
    domain = lax.axis_index("space")
    image = lax.axis_index("image")
    upper = lax.rem(domain + 1, n_space)
    lower = lax.rem(domain + n_space - 1, n_space)
    following = lax.rem(image + 1, n_image)
    previous = lax.rem(image + n_image - 1, n_image)
    atoms, per_atom = nb_ref.shape
    ext = 3 * atoms
    chunks, pairs = oh.shape[0], oh.shape[1]
    basis = fin_ref.shape[1]
    channels = emb_ref.shape[1]

    barrier = pltpu.get_barrier_semaphore()
    for i in range(1, n_space):
        pl.semaphore_signal(
            barrier, inc=1, device_id={"space": lax.rem(domain + i, n_space)}, device_id_type=MESH
        )
    for i in range(1, n_image):
        pl.semaphore_signal(
            barrier, inc=1, device_id={"image": lax.rem(image + i, n_image)}, device_id_type=MESH
        )

    def remote(src, dst, slot, where):
        return pltpu.make_async_remote_copy(
            src_ref=src, dst_ref=dst, send_sem=send.at[slot], recv_sem=recv.at[slot],
            device_id=where, device_id_type=MESH,
        )

    def spread(src, dst, out_sem, in_sem, axis, me, count):
        copies = []
        for i in range(1, count):
            copies.append(
                pltpu.make_async_remote_copy(
                    src_ref=src, dst_ref=dst.at[me], send_sem=out_sem.at[i], recv_sem=in_sem.at[me],
                    device_id={axis: lax.rem(me + i, count)}, device_id_type=MESH,
                )
            )
        for copy in copies:
            copy.start()
        dst[me] = src[...]

        def finish():
            for i in range(1, count):
                other = lax.rem(me + i, count)
                pltpu.make_async_remote_copy(
                    src_ref=src, dst_ref=dst.at[other], send_sem=out_sem.at[i],
                    recv_sem=in_sem.at[other], device_id={axis: other}, device_id_type=MESH,
                ).wait_recv()
            for copy in copies:
                copy.wait_send()

        return finish

    pos8[...] = jnp.zeros_like(pos8)
    pos8[0:3, :] = pos_ref[0]
    here = pos8[...]
    part_a = here.astype(BF16).astype(F32)
    rest = here - part_a
    part_b = rest.astype(BF16).astype(F32)
    part_c = rest - part_b
    parts = jnp.concatenate([part_a, part_b, part_c, jnp.zeros_like(here)], axis=0).astype(BF16)
    coord[0] = parts
    atom_rows = lax.broadcasted_iota(jnp.int32, (atoms, atoms), 0)
    embed = emb_ref[...]
    ext_emb[0:atoms, :] = embed
    for side, ids in ((0, up_ref), (1, down_ref)):
        picked = jnp.where(atom_rows == ids[...], 1.0, 0.0)
        sel_t[side] = picked.astype(BF16)
        sel[side] = picked.T.astype(BF16)
        coord_src[side] = dot(parts, sel_t[side]).astype(BF16)
        emb_src[side] = dot(sel[side], embed).astype(BF16)

    pl.semaphore_wait(barrier, n_space + n_image - 2)
    to_up, to_down = {"space": upper}, {"space": lower}
    coord_copies = [
        remote(coord_src.at[0], coord.at[1], 0, to_up),
        remote(coord_src.at[1], coord.at[2], 1, to_down),
    ]
    emb_copies = [
        remote(emb_src.at[0], ext_emb.at[pl.ds(atoms, atoms)], 2, to_up),
        remote(emb_src.at[1], ext_emb.at[pl.ds(2 * atoms, atoms)], 3, to_down),
    ]
    image_copies = [
        remote(pos8, prev8, 4, {"image": following}),
        remote(pos8, next8, 5, {"image": previous}),
    ]
    for copy in coord_copies + emb_copies + image_copies:
        copy.start()

    nb = nb_ref[...]
    nb_t[...] = nb.T
    ext_lane = lax.broadcasted_iota(jnp.int32, (atoms, ext), 1)
    ext_row = lax.broadcasted_iota(jnp.int32, (ext, pairs), 0)
    per_chunk = pairs // atoms
    for k in range(per_atom):
        c, r = k // per_chunk, k % per_chunk
        oh[c, r * atoms : (r + 1) * atoms, :] = onehot(nb[:, k : k + 1] == ext_lane)

    def slot_row(c):
        return jnp.concatenate(
            [nb_t[pl.ds(c * per_chunk + r, 1), :] for r in range(per_chunk)], axis=1
        )

    def build(c, carry):
        oht[c] = onehot(slot_row(c) == ext_row)
        return carry

    lax.fori_loop(0, chunks, build, 0)
    for layer in range(2):
        high, low = split_two(fin_ref[layer])
        lanes = slice(layer * channels, (layer + 1) * channels)
        w_in[:, lanes] = jnp.concatenate([high, high, low], axis=0)
        w_back[layer] = jnp.concatenate([high, low], axis=0)

    for copy in coord_copies + emb_copies:
        copy.wait_recv()

    low_shift = jnp.where(domain == 0, -n_space, 0).astype(F32)
    high_shift = jnp.where(domain == n_space - 1, n_space, 0).astype(F32)
    all_coord = jnp.concatenate([coord[0], coord[1], coord[2]], axis=1)
    here_wide = jnp.concatenate([here] * per_chunk, axis=1)
    first_row = lax.broadcasted_iota(jnp.int32, (8, pairs), 0) == 0
    centres = lax.broadcasted_iota(jnp.int32, (basis, pairs), 0).astype(F32) * (
        BASIS_REACH / (basis - 1)
    )
    ext_embed = ext_emb[...]
    fout_one, fout_two = fout_ref[0], fout_ref[1]

    def fold(values):
        total = values[0:atoms]
        for r in range(1, per_chunk):
            total = total + values[r * atoms : (r + 1) * atoms]
        return total

    def repeat(values):
        return jnp.concatenate([values] * per_chunk, axis=0)

    def layer_one(c, total):
        found = dot(all_coord, oht[c])
        slots = slot_row(c)
        shift = jnp.where(
            slots >= 2 * atoms, high_shift, jnp.where(slots >= atoms, low_shift, 0.0)
        )
        there = found[0:8] + found[8:16] + found[16:24]
        vec = there + jnp.where(first_row, shift, 0.0) - here_wide
        pv_all[c] = vec
        sq_dist = jnp.sum(vec * vec, axis=0, keepdims=True)
        scaled = (sq_dist - centres) * (1.0 / BASIS_WIDTH)
        radial = jnp.exp(-scaled * scaled)
        slope_all[c] = radial * (-2.0 / BASIS_WIDTH) * scaled
        high, low = split_two(radial)
        pre = dot_tn(jnp.concatenate([high, low, high], axis=0), w_in[...])
        pre_two[c] = pre[:, channels:]
        pre_one = pre[:, :channels]
        sig = gate(pre_one)
        act = pre_one * sig
        ds_one[c] = (sig + act * (1.0 - sig)).astype(BF16)
        filt = dot(act.astype(BF16), fout_one)
        rows = dot(oh[c], ext_embed)
        rows_one[c] = rows.astype(BF16)
        return total + fold(filt * rows)

    zeros = jnp.zeros((atoms, channels), F32)
    msg_one = lax.fori_loop(0, chunks, layer_one, zeros)
    upd_one = dot(msg_one.astype(BF16), uw_ref[0])
    sig_one = gate(upd_one)
    act_one = upd_one * sig_one
    slope_one = sig_one + act_one * (1.0 - sig_one)
    hidden = (embed.astype(F32) + act_one).astype(BF16)
    ext_hid[0:atoms, :] = hidden
    hid_src[0] = dot(sel[0], hidden).astype(BF16)
    hid_src[1] = dot(sel[1], hidden).astype(BF16)
    hid_copies = [
        remote(hid_src.at[0], ext_hid.at[pl.ds(atoms, atoms)], 6, to_up),
        remote(hid_src.at[1], ext_hid.at[pl.ds(2 * atoms, atoms)], 7, to_down),
    ]
    for copy in hid_copies:
        copy.start()

    for copy in image_copies:
        copy.wait_recv()
    ahead = jnp.where(image == n_image - 1, 0.0, next8[...]) - here
    behind = here - jnp.where(image == 0, 0.0, prev8[...])
    row8 = lax.broadcasted_iota(jnp.int32, (8, atoms), 0)

    def place(values):
        block = jnp.zeros((8, atoms), F32)
        for r, value in enumerate(values):
            block = jnp.where(row8 == r, value, block)
        return block

    def rows_sum(values):
        return jnp.sum(values, axis=0, keepdims=True)

    norm_src[...] = place([rows_sum(ahead * ahead), rows_sum(behind * behind)])
    norm_done = spread(norm_src, norm_in, norm_send, norm_recv, "space", domain, n_space)

    def filter_two(c, carry):
        pre = pre_two[c]
        sig = gate(pre)
        act = pre * sig
        ds_two[c] = (sig + act * (1.0 - sig)).astype(BF16)
        filt_two[c] = dot(act.astype(BF16), fout_two)
        return carry

    lax.fori_loop(0, chunks, filter_two, 0)
    for copy in hid_copies:
        copy.wait_recv()
    ext_hidden = ext_hid[...]

    def layer_two(c, total):
        rows = dot(oh[c], ext_hidden)
        rows_two[c] = rows.astype(BF16)
        return total + fold(filt_two[c] * rows)

    msg_two = lax.fori_loop(0, chunks, layer_two, zeros)
    upd_two = dot(msg_two.astype(BF16), uw_ref[1])
    sig_two = gate(upd_two)
    act_two = upd_two * sig_two
    readout = read_ref[...]
    energy_row = rows_sum(act_two * readout)
    dupd_two = ((sig_two + act_two * (1.0 - sig_two)) * readout).astype(BF16)
    dmsg_two = dot_nt(dupd_two, uw_ref[1])

    grad_all[...] = jnp.zeros_like(grad_all)

    def scatter_two(c, carry):
        source = (filt_two[c] * repeat(dmsg_two)).astype(BF16)
        grad_all[...] += dot(oht[c], source)
        return carry

    lax.fori_loop(0, chunks, scatter_two, 0)
    grad_src[0] = grad_all[atoms : 2 * atoms, :].astype(BF16)
    grad_src[1] = grad_all[2 * atoms : 3 * atoms, :].astype(BF16)
    grad_copies = [
        remote(grad_src.at[0], grad_in.at[0], 8, to_down),
        remote(grad_src.at[1], grad_in.at[1], 9, to_up),
    ]
    for copy in grad_copies:
        copy.start()

    def back(dmsg, rows, weight, slope, layer):
        dfilt = (repeat(dmsg) * rows.astype(F32)).astype(BF16)
        dact = dot_nt(dfilt, weight)
        dpre = (dact * slope.astype(F32)).astype(BF16)
        both = dot_nt(w_back[layer], dpre)
        return both[:basis] + both[basis:]

    def back_two(c, carry):
        drad[c] = back(dmsg_two, rows_two[c], fout_two, ds_two[c], 1)
        return carry

    lax.fori_loop(0, chunks, back_two, 0)
    for copy in grad_copies:
        copy.wait_recv()
    dhidden = grad_all[0:atoms, :] + dot(sel_t[0], grad_in[0]) + dot(sel_t[1], grad_in[1])
    dupd_one = (dhidden * slope_one).astype(BF16)
    dmsg_one = dot_nt(dupd_one, uw_ref[0])

    def back_one(c, carry):
        own, scattered = carry
        dradial = drad[c] + back(dmsg_one, rows_one[c], fout_one, ds_one[c], 0)
        dsq = jnp.sum(dradial * slope_all[c], axis=0, keepdims=True)
        pair = (2.0 * dsq) * pv_all[c]
        for r in range(per_chunk):
            own = own + pair[:, r * atoms : (r + 1) * atoms]
        high = pair.astype(BF16).astype(F32)
        both = jnp.concatenate([high, pair - high], axis=0).astype(BF16)
        return own, scattered + dot(both, oh[c])

    own, scattered = lax.fori_loop(
        0, chunks, back_one, (jnp.zeros((8, atoms), F32), jnp.zeros((16, ext), F32))
    )
    scattered = scattered[0:8] + scattered[8:16]
    force_src[0] = scattered[:, atoms : 2 * atoms]
    force_src[1] = scattered[:, 2 * atoms : 3 * atoms]
    force_copies = [
        remote(force_src.at[0], force_in.at[0], 10, to_down),
        remote(force_src.at[1], force_in.at[1], 11, to_up),
    ]
    for copy in force_copies:
        copy.start()

    norm_done()
    norm_sum = norm_in[0]
    for i in range(1, n_space):
        norm_sum = norm_sum + norm_in[i]
    norms = jnp.sqrt(jnp.sum(norm_sum, axis=1, keepdims=True) + EPSILON)
    ahead_norm, behind_norm = norms[0:1], norms[1:2]
    tangent = ahead / ahead_norm + behind / behind_norm
    tangent_row = rows_sum(tangent * tangent)
    speed = jnp.concatenate([vel_ref[0], jnp.zeros((5, atoms), F32)], axis=0)
    speed_row = rows_sum(speed * speed)
    spring_part = spring_ref[0, 0] * (ahead_norm - behind_norm)
    local_force = own - scattered[:, 0:atoms]
    for copy in force_copies:
        copy.wait_recv()

    def returned(side):
        ghost = force_in[side]
        high = ghost.astype(BF16).astype(F32)
        both = dot(jnp.concatenate([high, ghost - high], axis=0).astype(BF16), sel[side])
        return both[0:8] + both[8:16]

    forces = local_force - returned(0) - returned(1)
    sum_src[...] = place(
        [
            rows_sum(forces * forces), rows_sum(forces * tangent), tangent_row, energy_row,
            speed_row,
        ]
    )
    sum_done = spread(sum_src, sum_in, sum_send, sum_recv, "space", domain, n_space)
    sum_done()
    sums = sum_in[0]
    for i in range(1, n_space):
        sums = sums + sum_in[i]
    sums = jnp.sum(sums, axis=1, keepdims=True)
    force_sq, along, tangent_sq = sums[0:1], sums[1:2], sums[2:3]
    energy_ref[...] = sums[3:4]
    scale = 1.0 / jnp.sqrt(tangent_sq + EPSILON)
    parallel = along * scale
    unit_sq = tangent_sq * scale * scale
    climbing = climb_ref[0] > 0
    take = jnp.where(climbing, 2.0 * parallel, parallel - spring_part)
    movable = jnp.where((image > 0) & (image < n_image - 1), 1.0, 0.0)
    band_sq = jnp.maximum(force_sq - 2.0 * take * parallel + take * take * unit_sq, 0.0)
    band_src[...] = place([band_sq * movable, sums[4:5] * movable])
    band_done = spread(band_src, band_in, band_send, band_recv, "image", image, n_image)
    band_force = (forces - take * (tangent * scale)) * movable
    band_done()
    totals = band_in[0]
    for i in range(1, n_image):
        totals = totals + band_in[i]
    totals = jnp.sqrt(totals + EPSILON)
    force_norm, speed_norm = totals[0:1], totals[1:2]
    mixing = mix_ref[0, 0]
    time_step = step_ref[0, 0]
    mixed = (1.0 - mixing) * speed + mixing * (speed_norm / force_norm) * band_force
    kept = jnp.where(reset_ref[0] > 0, 0.0, mixed)
    new_speed = (kept + time_step * band_force) * movable
    newvel_ref[0] = new_speed[0:3]
    newpos_ref[0] = (here + time_step * new_speed)[0:3]
    for copy in (
        coord_copies + emb_copies + image_copies + hid_copies + grad_copies + force_copies
    ):
        copy.wait_send()


def per_device(
    n_space, n_image,
    positions, velocity, embed, neighbours, send_up, send_down, climb, reset,
    filter_in, filter_out, update_weight, readout, spring, time_step, mixing,
):
    atoms, per_atom = neighbours.shape
    channels = embed.shape[1]
    basis = filter_in.shape[1]
    per_chunk = 2
    chunks, pairs = per_atom // per_chunk, per_chunk * atoms
    ext = 3 * atoms
    vmem = pl.BlockSpec(memory_space=pltpu.VMEM)
    smem = pl.BlockSpec(memory_space=pltpu.SMEM)
    dma = pltpu.SemaphoreType.DMA
    scratch = [
        pltpu.VMEM((8, atoms), F32),
        pltpu.VMEM((8, atoms), F32),
        pltpu.VMEM((8, atoms), F32),
        pltpu.VMEM((3, 32, atoms), BF16),
        pltpu.VMEM((2, 32, atoms), BF16),
        pltpu.VMEM((ext, channels), BF16),
        pltpu.VMEM((2, atoms, channels), BF16),
        pltpu.VMEM((ext, channels), BF16),
        pltpu.VMEM((2, atoms, channels), BF16),
        pltpu.VMEM((ext, channels), F32),
        pltpu.VMEM((2, atoms, channels), BF16),
        pltpu.VMEM((2, atoms, channels), BF16),
        pltpu.VMEM((2, 8, atoms), F32),
        pltpu.VMEM((2, 8, atoms), F32),
        pltpu.VMEM((2, atoms, atoms), BF16),
        pltpu.VMEM((2, atoms, atoms), BF16),
        pltpu.VMEM((chunks, pairs, ext), BF16),
        pltpu.VMEM((chunks, ext, pairs), BF16),
        pltpu.VMEM((per_atom, atoms), jnp.int32),
        pltpu.VMEM((chunks, 8, pairs), F32),
        pltpu.VMEM((chunks, basis, pairs), F32),
        pltpu.VMEM((chunks, pairs, channels), F32),
        pltpu.VMEM((chunks, pairs, channels), BF16),
        pltpu.VMEM((chunks, pairs, channels), BF16),
        pltpu.VMEM((chunks, pairs, channels), BF16),
        pltpu.VMEM((chunks, pairs, channels), BF16),
        pltpu.VMEM((chunks, pairs, channels), F32),
        pltpu.VMEM((chunks, basis, pairs), F32),
        pltpu.VMEM((3 * basis, 2 * channels), BF16),
        pltpu.VMEM((2, 2 * basis, channels), BF16),
        pltpu.VMEM((8, atoms), F32),
        pltpu.VMEM((n_space, 8, atoms), F32),
        pltpu.VMEM((8, atoms), F32),
        pltpu.VMEM((n_space, 8, atoms), F32),
        pltpu.VMEM((8, atoms), F32),
        pltpu.VMEM((n_image, 8, atoms), F32),
        dma((12,)), dma((12,)),
        dma((n_space,)), dma((n_space,)),
        dma((n_space,)), dma((n_space,)),
        dma((n_image,)), dma((n_image,)),
    ]
    new_pos, new_vel, energy = pl.pallas_call(
        functools.partial(body, n_space, n_image),
        out_shape=(
            jax.ShapeDtypeStruct(positions.shape, F32),
            jax.ShapeDtypeStruct(velocity.shape, F32),
            jax.ShapeDtypeStruct((1, 1), F32),
        ),
        in_specs=[vmem] * 6 + [smem] * 2 + [vmem] * 4 + [smem] * 3,
        out_specs=(vmem, vmem, vmem),
        scratch_shapes=scratch,
        compiler_params=pltpu.CompilerParams(
            collective_id=0, has_side_effects=True, vmem_limit_bytes=48 * 1024 * 1024
        ),
    )(
        positions, velocity, embed, neighbours, send_up.reshape(1, -1), send_down.reshape(1, -1),
        climb, reset, filter_in, filter_out, update_weight, readout.reshape(1, -1),
        spring.reshape(1, 1), time_step.reshape(1, 1), mixing.reshape(1, 1),
    )
    return new_pos, new_vel, energy.reshape(1)


def solution(mesh):
    placed = (
        P("image", None, "space"), P("image", None, "space"), P("space", None), P("space", None),
        P("space"), P("space"), P("image"), P("image"), P(), P(), P(), P(), P(), P(), P(),
    )
    return jax.shard_map(
        functools.partial(per_device, mesh.shape["space"], mesh.shape["image"]),
        mesh=mesh,
        in_specs=placed,
        out_specs=(P("image", None, "space"), P("image", None, "space"), P("image")),
        check_vma=False,
    )
```

time: 280 us -> 67.8 us (0.24)
  blocking collectives: 97.3 us -> 0 us
  other arithmetic: 65.8 us -> 0 us
  Pallas kernels: 0 us -> 56.8 us
  local copies, waits for them, and re-layouts: 49.3 us -> 4.93 us
  starting transfers between devices: 29.6 us -> 0 us
  matrix products: 25.5 us -> 0 us
  between operations: 9.17 us -> 5.65 us
    psum x4 -> x0, blocking collectives: 97.3 us -> none  [the longest x1 37.1 us: per_device(): lax.psum((jnp.sum(band_force * band_force), jnp.where(movable, jnp.sum(sp...]
    pallas_call x0 -> x1, Pallas kernels: none -> 56.8 us  [per_device(): pl.pallas_call(functools.partial(body, n_space, n_image), out_shape=(jax....]
    scatter-add x6 -> x0, other arithmetic: 52.9 us -> none  [the longest x1 24.8 us: per_device(): jnp.zeros((3, atom_rows + 2 * ghost_rows), jnp.float32).at[:, slot_ids]]
    gather x11 -> x0, local copies, waits for them, and re-layouts: 43.5 us -> none  [the longest x1 14.9 us: per_device(): hidden_rows = ext_hidden[slot_ids]]
    ppermute x12 -> x0, starting transfers between devices: 29.6 us -> none  [the longest x6 24.1 us: with_halo(): lax.ppermute(head, axis, [((i + 1) % count, i) for i in range(ends)])]
    dot_general x13 -> x0, matrix products: 25.5 us -> none  [the longest x2 9.65 us: pair_filter(): lax.dot_general(radial_vals, weight_in, (((0,), (0,)), ((), ())), precisi...]
    reduce_sum x6 -> x0, other arithmetic: 5.25 us -> none  [the longest x1 1.34 us: per_device(): jnp.sum(band_force * band_force)]
  transfers between devices with their start and end apart: 12 -> 0, of which waited for: 2 -> 0; matrix products, arithmetic and copies ran while one was open for 13% -> 0% of each run, Pallas kernels for 0% -> 0%
where the time goes in v1:
time: 67.8 us; the launch traced here: 67.4 us
  Pallas kernels  56.8 us (84%)
  between operations  5.65 us (8%)
  local copies, waits for them, and re-layouts  4.93 us (7%)
    pallas_call x1, Pallas kernels, per_device(): pl.pallas_call(functools.partial(body, n_space, n_image), out_shape=(jax....  56.8 us
    unnamed x19, local copies, waits for them, and re-layouts  4.93 us

profile of v1, /device:TPU:0, one launch (start us, length us, event | category | flops | bytes accessed | tf_op | source)
XLA Modules:
  0.0 67.4 jit_solution(7857900116066483561)
XLA Ops:
  0.6 0.0 copy-start
  3.9 0.7 %copy.18.pos_ref = f32[1,3,128]{2,1,0:T(4,128)S(1)} copy(f32[1,3,128]{2,0,1:T(1,128)} %param.15) | data formatting | bytes 3072 | tf_op args[0]
  4.6 0.7 %copy.19.vel_ref = f32[1,3,128]{2,1,0:T(4,128)S(1)} copy(f32[1,3,128]{2,0,1:T(1,128)} %param.16) | data formatting | bytes 3072 | tf_op args[1]
  5.3 0.0 copy-start.2
  5.3 0.0 copy-start.4
  5.3 0.0 copy-start.5
  5.3 0.0 copy-start.6
  5.3 0.9 %copy.20.nb_ref = s32[128,32]{1,0:T(8,128)S(1)} copy(s32[128,32]{0,1:T(8,128)} %param.18) | data formatting | bytes 32768 | tf_op args[3]
  6.1 0.0 copy-done
  6.1 0.0 copy-done.2
  6.2 0.0 copy-done.4
  6.2 0.0 copy-done.5
  6.2 0.0 copy-done.6
  6.2 0.0 copy-start.1
  6.2 0.8 %copy-done.1 = bf16[2,128,128]{2,1,0:T(8,128)(2,1)S(1)} copy-done((bf16[2,128,128]{2,1,0:T(8,128)(2,1)S(1)}, bf16[2,128,128]{2,1,0:T(8,128)(2,1)}, u32[]{:S(2)}) %copy-start.1) | copy-done | bytes 65560
  7.0 0.0 copy-start.3
  7.0 0.7 %copy-done.3 = f32[2,16,128]{2,1,0:T(8,128)S(1)} copy-done((f32[2,16,128]{2,1,0:T(8,128)S(1)}, f32[2,16,128]{2,1,0:T(8,128)}, u32[]{:S(2)}) %copy-start.3) | copy-done | bytes 16408
  7.8 56.8 %shard_map.166 = (f32[1,3,128]{2,1,0:T(4,128)S(1)}, f32[1,3,128]{2,1,0:T(4,128)S(1)}, f32[1,1]{1,0:T(1,128)}) custom-call(f32[1,3,128]{2,1,0:T(4,128)S(1)} %copy.18.pos_ref, f32[1,3,128]{2,1,0:T(4,128)S(1)} %copy.19.vel_ref, bf16[128,128]{1,0:T(8,128)(2,1)S(1)} %copy-done.2, s32[128,32]{1,0:T(8,128)S(1)} %copy.20.nb_ref, s32[1,128]{1,0:T(1,128)S(1)} %bitcast.10, ...), custom_call_target="tpu_custom_call" | custom-call | tf_op jit(solution)/shard_map/pallas_call | solution.py:459
  64.6 0.6 copy.21
  65.1 0.6 copy.22
Async XLA Ops:
  0.6 5.5 %copy-start = (bf16[2,128,128]{2,1,0:T(8,128)(2,1)S(1)}, bf16[2,128,128]{2,1,0:T(8,128)(2,1)}, u32[]{:S(2)}) copy-start(bf16[2,128,128]{2,1,0:T(8,128)(2,1)} %fout_ref.1) | copy-start | bytes 196612
  5.3 0.9 %copy-start.2 = (bf16[128,128]{1,0:T(8,128)(2,1)S(1)}, bf16[128,128]{1,0:T(8,128)(2,1)}, u32[]{:S(2)}) copy-start(bf16[128,128]{1,0:T(8,128)(2,1)} %emb_ref.1) | copy-start | bytes 98308
  5.3 0.9 %copy-start.4 = (s32[128]{0:T(128)S(1)}, s32[128]{0:T(128)}, u32[]{:S(2)}) copy-start(s32[128]{0:T(128)} %param.19) | copy-start | bytes 1540
  5.3 0.9 %copy-start.5 = (s32[128]{0:T(128)S(1)}, s32[128]{0:T(128)}, u32[]{:S(2)}) copy-start(s32[128]{0:T(128)} %param.20) | copy-start | bytes 1540
  5.3 0.9 %copy-start.6 = (f32[128]{0:T(128)S(1)}, f32[128]{0:T(128)}, u32[]{:S(2)}) copy-start(f32[128]{0:T(128)} %param.26) | copy-start | bytes 1540
  6.2 0.8 %copy-start.1 = (bf16[2,128,128]{2,1,0:T(8,128)(2,1)S(1)}, bf16[2,128,128]{2,1,0:T(8,128)(2,1)}, u32[]{:S(2)}) copy-start(bf16[2,128,128]{2,1,0:T(8,128)(2,1)} %uw_ref.1) | copy-start | bytes 196612
  7.0 0.7 %copy-start.3 = (f32[2,16,128]{2,1,0:T(8,128)S(1)}, f32[2,16,128]{2,1,0:T(8,128)}, u32[]{:S(2)}) copy-start(f32[2,16,128]{2,1,0:T(8,128)} %fin_ref.1) | copy-start | bytes 49156

commit v2 on v1

--- a/solution.py
+++ b/solution.py
@@ -42,12 +42,14 @@
 
 def body(
     n_space, n_image,
-    pos_ref, vel_ref, emb_ref, nb_ref, up_ref, down_ref, climb_ref, reset_ref,
-    fin_ref, fout_ref, uw_ref, read_ref, spring_ref, step_ref, mix_ref,
+    pos_hbm, vel_hbm, emb_hbm, nb_hbm, up_hbm, down_hbm, climb_hbm, reset_hbm,
+    fin_hbm, fout_hbm, uw_hbm, read_hbm, spring_hbm, step_hbm, mix_hbm,
     newpos_ref, newvel_ref, energy_ref,
+    pos_ref, vel_ref, emb_ref, nb_t, up_ref, down_ref, climb_ref, reset_ref,
+    fin_ref, fout_ref, uw_ref, read_ref, spring_ref, step_ref, mix_ref, fetch_sem,
     pos8, prev8, next8, coord, coord_src, ext_emb, emb_src, ext_hid, hid_src,
     grad_all, grad_src, grad_in, force_src, force_in,
-    sel, sel_t, oh, oht, nb_t, pv_all, slope_all, pre_two, ds_one, ds_two,
+    sel, sel_t, oh, oht, pv_all, slope_all, pre_two, ds_one, ds_two,
     rows_one, rows_two, filt_two, drad, w_in, w_back,
     norm_src, norm_in, sum_src, sum_in, band_src, band_in,
     send, recv, norm_send, norm_recv, sum_send, sum_recv, band_send, band_recv,
@@ -58,11 +60,26 @@
     lower = lax.rem(domain + n_space - 1, n_space)
     following = lax.rem(image + 1, n_image)
     previous = lax.rem(image + n_image - 1, n_image)
-    atoms, per_atom = nb_ref.shape
+    per_atom, atoms = nb_t.shape
     ext = 3 * atoms
     chunks, pairs = oh.shape[0], oh.shape[1]
     basis = fin_ref.shape[1]
     channels = emb_ref.shape[1]
+
+    sources = (
+        pos_hbm, vel_hbm, emb_hbm, nb_hbm, up_hbm, down_hbm, climb_hbm, reset_hbm,
+        fin_hbm, fout_hbm, uw_hbm, read_hbm, spring_hbm, step_hbm, mix_hbm,
+    )
+    targets = (
+        pos_ref, vel_ref, emb_ref, nb_t, up_ref, down_ref, climb_ref, reset_ref,
+        fin_ref, fout_ref, uw_ref, read_ref, spring_ref, step_ref, mix_ref,
+    )
+    fetches = [
+        pltpu.make_async_copy(source, target, fetch_sem.at[i])
+        for i, (source, target) in enumerate(zip(sources, targets))
+    ]
+    for i in (0, 4, 5, 2, 3, 8, 9, 10, 1, 11, 6, 7, 12, 13, 14):
+        fetches[i].start()
 
     barrier = pltpu.get_barrier_semaphore()
     for i in range(1, n_space):
@@ -105,8 +122,11 @@
 
         return finish
 
+    for i in (0, 4, 5, 2):
+        fetches[i].wait()
     pos8[...] = jnp.zeros_like(pos8)
-    pos8[0:3, :] = pos_ref[0]
+    for r in range(3):
+        pos8[r : r + 1, :] = pos_ref[r]
     here = pos8[...]
     part_a = here.astype(BF16).astype(F32)
     rest = here - part_a
@@ -141,8 +161,9 @@
     for copy in coord_copies + emb_copies + image_copies:
         copy.start()
 
-    nb = nb_ref[...]
-    nb_t[...] = nb.T
+    for i in (3, 8, 9, 10, 1, 11, 6, 7, 12, 13, 14):
+        fetches[i].wait()
+    nb = nb_t[...].T
     ext_lane = lax.broadcasted_iota(jnp.int32, (atoms, ext), 1)
     ext_row = lax.broadcasted_iota(jnp.int32, (ext, pairs), 0)
     per_chunk = pairs // atoms
@@ -159,7 +180,7 @@
         oht[c] = onehot(slot_row(c) == ext_row)
         return carry
 
-    lax.fori_loop(0, chunks, build, 0)
+    lax.fori_loop(0, chunks, build, 0, unroll=2)
     for layer in range(2):
         high, low = split_two(fin_ref[layer])
         lanes = slice(layer * channels, (layer + 1) * channels)
@@ -215,7 +236,7 @@
         return total + fold(filt * rows)
 
     zeros = jnp.zeros((atoms, channels), F32)
-    msg_one = lax.fori_loop(0, chunks, layer_one, zeros)
+    msg_one = lax.fori_loop(0, chunks, layer_one, zeros, unroll=4)
     upd_one = dot(msg_one.astype(BF16), uw_ref[0])
     sig_one = gate(upd_one)
     act_one = upd_one * sig_one
@@ -257,7 +278,7 @@
         filt_two[c] = dot(act.astype(BF16), fout_two)
         return carry
 
-    lax.fori_loop(0, chunks, filter_two, 0)
+    lax.fori_loop(0, chunks, filter_two, 0, unroll=4)
     for copy in hid_copies:
         copy.wait_recv()
     ext_hidden = ext_hid[...]
@@ -267,7 +288,7 @@
         rows_two[c] = rows.astype(BF16)
         return total + fold(filt_two[c] * rows)
 
-    msg_two = lax.fori_loop(0, chunks, layer_two, zeros)
+    msg_two = lax.fori_loop(0, chunks, layer_two, zeros, unroll=4)
     upd_two = dot(msg_two.astype(BF16), uw_ref[1])
     sig_two = gate(upd_two)
     act_two = upd_two * sig_two
@@ -277,13 +298,20 @@
     dmsg_two = dot_nt(dupd_two, uw_ref[1])
 
     grad_all[...] = jnp.zeros_like(grad_all)
-
-    def scatter_two(c, carry):
-        source = (filt_two[c] * repeat(dmsg_two)).astype(BF16)
-        grad_all[...] += dot(oht[c], source)
+    group = 4
+
+    def scatter_two(g, carry):
+        picks, sources = [], []
+        for i in range(group):
+            c = g * group + i
+            picks.append(oht[c])
+            sources.append((filt_two[c] * repeat(dmsg_two)).astype(BF16))
+        grad_all[...] += dot(
+            jnp.concatenate(picks, axis=1), jnp.concatenate(sources, axis=0)
+        )
         return carry
 
-    lax.fori_loop(0, chunks, scatter_two, 0)
+    lax.fori_loop(0, chunks // group, scatter_two, 0)
     grad_src[0] = grad_all[atoms : 2 * atoms, :].astype(BF16)
     grad_src[1] = grad_all[2 * atoms : 3 * atoms, :].astype(BF16)
     grad_copies = [
@@ -304,7 +332,7 @@
         drad[c] = back(dmsg_two, rows_two[c], fout_two, ds_two[c], 1)
         return carry
 
-    lax.fori_loop(0, chunks, back_two, 0)
+    lax.fori_loop(0, chunks, back_two, 0, unroll=4)
     for copy in grad_copies:
         copy.wait_recv()
     dhidden = grad_all[0:atoms, :] + dot(sel_t[0], grad_in[0]) + dot(sel_t[1], grad_in[1])
@@ -323,7 +351,8 @@
         return own, scattered + dot(both, oh[c])
 
     own, scattered = lax.fori_loop(
-        0, chunks, back_one, (jnp.zeros((8, atoms), F32), jnp.zeros((16, ext), F32))
+        0, chunks, back_one, (jnp.zeros((8, atoms), F32), jnp.zeros((16, ext), F32)),
+        unroll=4,
     )
     scattered = scattered[0:8] + scattered[8:16]
     force_src[0] = scattered[:, atoms : 2 * atoms]
@@ -343,9 +372,9 @@
     ahead_norm, behind_norm = norms[0:1], norms[1:2]
     tangent = ahead / ahead_norm + behind / behind_norm
     tangent_row = rows_sum(tangent * tangent)
-    speed = jnp.concatenate([vel_ref[0], jnp.zeros((5, atoms), F32)], axis=0)
+    speed = place([vel_ref[r] for r in range(3)])
     speed_row = rows_sum(speed * speed)
-    spring_part = spring_ref[0, 0] * (ahead_norm - behind_norm)
+    spring_part = spring_ref[0] * (ahead_norm - behind_norm)
     local_force = own - scattered[:, 0:atoms]
     for copy in force_copies:
         copy.wait_recv()
@@ -387,13 +416,15 @@
         totals = totals + band_in[i]
     totals = jnp.sqrt(totals + EPSILON)
     force_norm, speed_norm = totals[0:1], totals[1:2]
-    mixing = mix_ref[0, 0]
-    time_step = step_ref[0, 0]
+    mixing = mix_ref[0]
+    time_step = step_ref[0]
     mixed = (1.0 - mixing) * speed + mixing * (speed_norm / force_norm) * band_force
     kept = jnp.where(reset_ref[0] > 0, 0.0, mixed)
     new_speed = (kept + time_step * band_force) * movable
-    newvel_ref[0] = new_speed[0:3]
-    newpos_ref[0] = (here + time_step * new_speed)[0:3]
+    new_place = here + time_step * new_speed
+    for r in range(3):
+        newvel_ref[r] = new_speed[r : r + 1]
+        newpos_ref[r] = new_place[r : r + 1]
     for copy in (
         coord_copies + emb_copies + image_copies + hid_copies + grad_copies + force_copies
     ):
@@ -412,9 +443,26 @@
     chunks, pairs = per_atom // per_chunk, per_chunk * atoms
     ext = 3 * atoms
     vmem = pl.BlockSpec(memory_space=pltpu.VMEM)
-    smem = pl.BlockSpec(memory_space=pltpu.SMEM)
+    hbm = pl.BlockSpec(memory_space=pltpu.HBM)
     dma = pltpu.SemaphoreType.DMA
+    basis_shape = filter_in.shape
     scratch = [
+        pltpu.VMEM((3, 1, atoms), F32),
+        pltpu.VMEM((3, 1, atoms), F32),
+        pltpu.VMEM((atoms, channels), BF16),
+        pltpu.VMEM((per_atom, atoms), jnp.int32),
+        pltpu.VMEM((1, atoms), jnp.int32),
+        pltpu.VMEM((1, atoms), jnp.int32),
+        pltpu.SMEM((1,), jnp.int32),
+        pltpu.SMEM((1,), jnp.int32),
+        pltpu.VMEM(basis_shape, F32),
+        pltpu.VMEM((2, channels, channels), BF16),
+        pltpu.VMEM((2, channels, channels), BF16),
+        pltpu.VMEM((1, channels), F32),
+        pltpu.SMEM((1,), F32),
+        pltpu.SMEM((1,), F32),
+        pltpu.SMEM((1,), F32),
+        dma((15,)),
         pltpu.VMEM((8, atoms), F32),
         pltpu.VMEM((8, atoms), F32),
         pltpu.VMEM((8, atoms), F32),
@@ -433,7 +481,6 @@
         pltpu.VMEM((2, atoms, atoms), BF16),
         pltpu.VMEM((chunks, pairs, ext), BF16),
         pltpu.VMEM((chunks, ext, pairs), BF16),
-        pltpu.VMEM((per_atom, atoms), jnp.int32),
         pltpu.VMEM((chunks, 8, pairs), F32),
         pltpu.VMEM((chunks, basis, pairs), F32),
         pltpu.VMEM((chunks, pairs, channels), F32),
@@ -459,22 +506,24 @@
     new_pos, new_vel, energy = pl.pallas_call(
         functools.partial(body, n_space, n_image),
         out_shape=(
-            jax.ShapeDtypeStruct(positions.shape, F32),
-            jax.ShapeDtypeStruct(velocity.shape, F32),
+            jax.ShapeDtypeStruct((3, 1, atoms), F32),
+            jax.ShapeDtypeStruct((3, 1, atoms), F32),
             jax.ShapeDtypeStruct((1, 1), F32),
         ),
-        in_specs=[vmem] * 6 + [smem] * 2 + [vmem] * 4 + [smem] * 3,
+        in_specs=[hbm] * 15,
         out_specs=(vmem, vmem, vmem),
         scratch_shapes=scratch,
         compiler_params=pltpu.CompilerParams(
-            collective_id=0, has_side_effects=True, vmem_limit_bytes=48 * 1024 * 1024
+            collective_id=0, has_side_effects=True, vmem_limit_bytes=60 * 1024 * 1024
         ),
     )(
-        positions, velocity, embed, neighbours, send_up.reshape(1, -1), send_down.reshape(1, -1),
-        climb, reset, filter_in, filter_out, update_weight, readout.reshape(1, -1),
-        spring.reshape(1, 1), time_step.reshape(1, 1), mixing.reshape(1, 1),
-    )
-    return new_pos, new_vel, energy.reshape(1)
+        jnp.transpose(positions, (1, 0, 2)), jnp.transpose(velocity, (1, 0, 2)), embed,
+        neighbours.T, send_up.reshape(1, -1), send_down.reshape(1, -1), climb, reset,
+        filter_in, filter_out, update_weight, readout.reshape(1, -1),
+        spring.reshape(1), time_step.reshape(1), mixing.reshape(1),
+    )
+    back = (1, 0, 2)
+    return jnp.transpose(new_pos, back), jnp.transpose(new_vel, back), energy.reshape(1)
 
 
 def solution(mesh):

time: 67.8 us -> 54.6 us (0.81)
  Pallas kernels: 56.8 us -> 46.9 us
  local copies, waits for them, and re-layouts: 4.93 us -> 1.85 us
    pallas_call x1, Pallas kernels: 56.8 us -> 46.9 us  [per_device(): pl.pallas_call(functools.partial(body, n_space, n_image), out_shape=(jax....]
    unnamed x19 -> x6, local copies, waits for them, and re-layouts: 4.93 us -> 1.85 us
where the time goes in v2:
time: 54.6 us; the launch traced here: 54.3 us
  Pallas kernels  46.9 us (86%)
  between operations  5.63 us (10%)
  local copies, waits for them, and re-layouts  1.85 us (3%)
    pallas_call x1, Pallas kernels, per_device(): pl.pallas_call(functools.partial(body, n_space, n_image), out_shape=(jax....  46.9 us
    unnamed x6, local copies, waits for them, and re-layouts  1.85 us

profile of v2, /device:TPU:0, one launch (start us, length us, event | category | flops | bytes accessed | tf_op | source)
XLA Modules:
  0.0 54.3 jit_solution(10665362529227427034)
XLA Ops:
  3.9 46.9 %shard_map.166 = (f32[3,1,128]{2,1,0:T(1,128)}, f32[3,1,128]{2,1,0:T(1,128)}, f32[1,1]{1,0:T(1,128)}) custom-call(f32[3,1,128]{2,1,0:T(1,128)} %bitcast.16, f32[3,1,128]{2,1,0:T(1,128)} %bitcast.17, bf16[128,128]{1,0:T(8,128)(2,1)} %emb_hbm.1, s32[32,128]{1,0:T(8,128)} %bitcast.15, s32[1,128]{1,0:T(1,128)} %bitcast.20, s32[1,128]{1,0:T(1,128)} %bitcast.21, ...), custom_call_target="tpu_custom_call" | custom-call | tf_op jit(solution)/shard_map/pallas_call | solution.py:506
  50.7 0.0 copy-start.1
  50.7 0.7 %copy-done.1 = f32[3,1,128]{2,1,0:T(1,128)S(1)} copy-done((f32[3,1,128]{2,1,0:T(1,128)S(1)}, f32[3,1,128]{2,1,0:T(1,128)}, u32[]{:S(2)}) %copy-start.1) | copy-done | bytes 1560
  51.4 0.0 copy-start
  51.4 0.6 %copy.26 = f32[1,3,128]{2,0,1:T(1,128)} copy(f32[1,3,128]{2,0,1:T(1,128)S(1)} %bitcast.19) | data formatting | bytes 3072
  52.0 0.1 copy-done
  52.0 0.6 %copy.27 = f32[1,3,128]{2,0,1:T(1,128)} copy(f32[1,3,128]{2,0,1:T(1,128)S(1)} %bitcast.18) | data formatting | bytes 3072
Async XLA Ops:
  50.7 0.7 %copy-start.1 = (f32[3,1,128]{2,1,0:T(1,128)S(1)}, f32[3,1,128]{2,1,0:T(1,128)}, u32[]{:S(2)}) copy-start(f32[3,1,128]{2,1,0:T(1,128)} %get-tuple-element.6) | copy-start | bytes 4612
  51.4 0.6 %copy-start = (f32[3,1,128]{2,1,0:T(1,128)S(1)}, f32[3,1,128]{2,1,0:T(1,128)}, u32[]{:S(2)}) copy-start(f32[3,1,128]{2,1,0:T(1,128)} %get-tuple-element.7) | copy-start | bytes 4612

commit v3 on v2

--- a/solution.py
+++ b/solution.py
@@ -144,6 +144,20 @@
         coord_src[side] = dot(parts, sel_t[side]).astype(BF16)
         emb_src[side] = dot(sel[side], embed).astype(BF16)
 
+    fetches[3].wait()
+    per_chunk = pairs // atoms
+    ext_lane = lax.broadcasted_iota(jnp.int32, (atoms, ext), 1)
+    nb_wide = jnp.concatenate(
+        [nb_t[...], jnp.zeros((atoms - per_atom, atoms), jnp.int32)], axis=0
+    ).T
+
+    def build_rows(c, slots):
+        for r in range(per_chunk):
+            oh[c, r * atoms : (r + 1) * atoms, :] = onehot(slots[:, 0:1] == ext_lane)
+            slots = pltpu.roll(slots, atoms - 1, 1)
+        return slots
+
+    lax.fori_loop(0, chunks, build_rows, nb_wide, unroll=2)
     pl.semaphore_wait(barrier, n_space + n_image - 2)
     to_up, to_down = {"space": upper}, {"space": lower}
     coord_copies = [
@@ -161,16 +175,9 @@
     for copy in coord_copies + emb_copies + image_copies:
         copy.start()
 
-    for i in (3, 8, 9, 10, 1, 11, 6, 7, 12, 13, 14):
+    for i in (8, 9, 10, 1, 11, 6, 7, 12, 13, 14):
         fetches[i].wait()
-    nb = nb_t[...].T
-    ext_lane = lax.broadcasted_iota(jnp.int32, (atoms, ext), 1)
     ext_row = lax.broadcasted_iota(jnp.int32, (ext, pairs), 0)
-    per_chunk = pairs // atoms
-    for k in range(per_atom):
-        c, r = k // per_chunk, k % per_chunk
-        oh[c, r * atoms : (r + 1) * atoms, :] = onehot(nb[:, k : k + 1] == ext_lane)
-
     def slot_row(c):
         return jnp.concatenate(
             [nb_t[pl.ds(c * per_chunk + r, 1), :] for r in range(per_chunk)], axis=1
@@ -229,8 +236,9 @@
         pre_one = pre[:, :channels]
         sig = gate(pre_one)
         act = pre_one * sig
-        ds_one[c] = (sig + act * (1.0 - sig)).astype(BF16)
-        filt = dot(act.astype(BF16), fout_one)
+        sig, act = sig.astype(BF16), act.astype(BF16)
+        ds_one[c] = sig + act * (1.0 - sig)
+        filt = dot(act, fout_one)
         rows = dot(oh[c], ext_embed)
         rows_one[c] = rows.astype(BF16)
         return total + fold(filt * rows)
@@ -274,11 +282,12 @@
         pre = pre_two[c]
         sig = gate(pre)
         act = pre * sig
-        ds_two[c] = (sig + act * (1.0 - sig)).astype(BF16)
-        filt_two[c] = dot(act.astype(BF16), fout_two)
+        sig, act = sig.astype(BF16), act.astype(BF16)
+        ds_two[c] = sig + act * (1.0 - sig)
+        filt_two[c] = dot(act, fout_two)
         return carry
 
-    lax.fori_loop(0, chunks, filter_two, 0, unroll=4)
+    lax.fori_loop(0, chunks, filter_two, 0, unroll=8)
     for copy in hid_copies:
         copy.wait_recv()
     ext_hidden = ext_hid[...]
@@ -288,7 +297,7 @@
         rows_two[c] = rows.astype(BF16)
         return total + fold(filt_two[c] * rows)
 
-    msg_two = lax.fori_loop(0, chunks, layer_two, zeros, unroll=4)
+    msg_two = lax.fori_loop(0, chunks, layer_two, zeros, unroll=8)
     upd_two = dot(msg_two.astype(BF16), uw_ref[1])
     sig_two = gate(upd_two)
     act_two = upd_two * sig_two
@@ -322,22 +331,22 @@
         copy.start()
 
     def back(dmsg, rows, weight, slope, layer):
-        dfilt = (repeat(dmsg) * rows.astype(F32)).astype(BF16)
-        dact = dot_nt(dfilt, weight)
-        dpre = (dact * slope.astype(F32)).astype(BF16)
+        dact = dot_nt(repeat(dmsg) * rows, weight)
+        dpre = dact.astype(BF16) * slope
         both = dot_nt(w_back[layer], dpre)
         return both[:basis] + both[basis:]
 
     def back_two(c, carry):
-        drad[c] = back(dmsg_two, rows_two[c], fout_two, ds_two[c], 1)
+        drad[c] = back(dmsg_two_low, rows_two[c], fout_two, ds_two[c], 1)
         return carry
 
-    lax.fori_loop(0, chunks, back_two, 0, unroll=4)
+    dmsg_two_low = dmsg_two.astype(BF16)
+    lax.fori_loop(0, chunks, back_two, 0, unroll=8)
     for copy in grad_copies:
         copy.wait_recv()
     dhidden = grad_all[0:atoms, :] + dot(sel_t[0], grad_in[0]) + dot(sel_t[1], grad_in[1])
     dupd_one = (dhidden * slope_one).astype(BF16)
-    dmsg_one = dot_nt(dupd_one, uw_ref[0])
+    dmsg_one = dot_nt(dupd_one, uw_ref[0]).astype(BF16)
 
     def back_one(c, carry):
         own, scattered = carry

time: 54.6 us -> 57.2 us (1.048)
  Pallas kernels: 46.9 us -> 49.5 us
    pallas_call x1, Pallas kernels: 46.9 us -> 49.5 us  [per_device(): pl.pallas_call(functools.partial(body, n_space, n_image), out_shape=(jax....]
where the time goes in v3:
time: 57.2 us; the launch traced here: 56.9 us
  Pallas kernels  49.5 us (87%)
  between operations  5.63 us (10%)
  local copies, waits for them, and re-layouts  1.85 us (3%)
    pallas_call x1, Pallas kernels, per_device(): pl.pallas_call(functools.partial(body, n_space, n_image), out_shape=(jax....  49.5 us
    unnamed x6, local copies, waits for them, and re-layouts  1.85 us

profile of v3, /device:TPU:0, one launch (start us, length us, event | category | flops | bytes accessed | tf_op | source)
XLA Modules:
  0.0 56.9 jit_solution(9341536291442829795)
XLA Ops:
  3.9 49.5 %shard_map.166 = (f32[3,1,128]{2,1,0:T(1,128)}, f32[3,1,128]{2,1,0:T(1,128)}, f32[1,1]{1,0:T(1,128)}) custom-call(f32[3,1,128]{2,1,0:T(1,128)} %bitcast.16, f32[3,1,128]{2,1,0:T(1,128)} %bitcast.17, bf16[128,128]{1,0:T(8,128)(2,1)} %emb_hbm.1, s32[32,128]{1,0:T(8,128)} %bitcast.15, s32[1,128]{1,0:T(1,128)} %bitcast.20, s32[1,128]{1,0:T(1,128)} %bitcast.21, ...), custom_call_target="tpu_custom_call" | custom-call | tf_op jit(solution)/shard_map/pallas_call | solution.py:515
  53.3 0.0 copy-start.1
  53.3 0.7 %copy-done.1 = f32[3,1,128]{2,1,0:T(1,128)S(1)} copy-done((f32[3,1,128]{2,1,0:T(1,128)S(1)}, f32[3,1,128]{2,1,0:T(1,128)}, u32[]{:S(2)}) %copy-start.1) | copy-done | bytes 1560
  54.0 0.0 copy-start
  54.0 0.6 copy.26
  54.6 0.1 copy-done
  54.6 0.6 copy.27
Async XLA Ops:
  53.3 0.7 %copy-start.1 = (f32[3,1,128]{2,1,0:T(1,128)S(1)}, f32[3,1,128]{2,1,0:T(1,128)}, u32[]{:S(2)}) copy-start(f32[3,1,128]{2,1,0:T(1,128)} %get-tuple-element.6) | copy-start | bytes 4612
  54.0 0.6 %copy-start = (f32[3,1,128]{2,1,0:T(1,128)S(1)}, f32[3,1,128]{2,1,0:T(1,128)}, u32[]{:S(2)}) copy-start(f32[3,1,128]{2,1,0:T(1,128)} %get-tuple-element.7) | copy-start | bytes 4612

commit v4 on v2

--- a/solution.py
+++ b/solution.py
@@ -164,13 +164,12 @@
     for i in (3, 8, 9, 10, 1, 11, 6, 7, 12, 13, 14):
         fetches[i].wait()
     nb = nb_t[...].T
+    per_chunk = pairs // atoms
     ext_lane = lax.broadcasted_iota(jnp.int32, (atoms, ext), 1)
-    ext_row = lax.broadcasted_iota(jnp.int32, (ext, pairs), 0)
-    per_chunk = pairs // atoms
     for k in range(per_atom):
         c, r = k // per_chunk, k % per_chunk
         oh[c, r * atoms : (r + 1) * atoms, :] = onehot(nb[:, k : k + 1] == ext_lane)
-
+    ext_row = lax.broadcasted_iota(jnp.int32, (ext, pairs), 0)
     def slot_row(c):
         return jnp.concatenate(
             [nb_t[pl.ds(c * per_chunk + r, 1), :] for r in range(per_chunk)], axis=1
@@ -180,7 +179,7 @@
         oht[c] = onehot(slot_row(c) == ext_row)
         return carry
 
-    lax.fori_loop(0, chunks, build, 0, unroll=2)
+    lax.fori_loop(0, chunks, build, 0, unroll=1)
     for layer in range(2):
         high, low = split_two(fin_ref[layer])
         lanes = slice(layer * channels, (layer + 1) * channels)
@@ -229,14 +228,15 @@
         pre_one = pre[:, :channels]
         sig = gate(pre_one)
         act = pre_one * sig
-        ds_one[c] = (sig + act * (1.0 - sig)).astype(BF16)
-        filt = dot(act.astype(BF16), fout_one)
+        sig, act = sig.astype(BF16), act.astype(BF16)
+        ds_one[c] = sig + act * (1.0 - sig)
+        filt = dot(act, fout_one)
         rows = dot(oh[c], ext_embed)
         rows_one[c] = rows.astype(BF16)
         return total + fold(filt * rows)
 
     zeros = jnp.zeros((atoms, channels), F32)
-    msg_one = lax.fori_loop(0, chunks, layer_one, zeros, unroll=4)
+    msg_one = lax.fori_loop(0, chunks, layer_one, zeros, unroll=2)
     upd_one = dot(msg_one.astype(BF16), uw_ref[0])
     sig_one = gate(upd_one)
     act_one = upd_one * sig_one
@@ -274,8 +274,9 @@
         pre = pre_two[c]
         sig = gate(pre)
         act = pre * sig
-        ds_two[c] = (sig + act * (1.0 - sig)).astype(BF16)
-        filt_two[c] = dot(act.astype(BF16), fout_two)
+        sig, act = sig.astype(BF16), act.astype(BF16)
+        ds_two[c] = sig + act * (1.0 - sig)
+        filt_two[c] = dot(act, fout_two)
         return carry
 
     lax.fori_loop(0, chunks, filter_two, 0, unroll=4)
@@ -298,7 +299,7 @@
     dmsg_two = dot_nt(dupd_two, uw_ref[1])
 
     grad_all[...] = jnp.zeros_like(grad_all)
-    group = 4
+    group = 2
 
     def scatter_two(g, carry):
         picks, sources = [], []
@@ -322,22 +323,22 @@
         copy.start()
 
     def back(dmsg, rows, weight, slope, layer):
-        dfilt = (repeat(dmsg) * rows.astype(F32)).astype(BF16)
-        dact = dot_nt(dfilt, weight)
-        dpre = (dact * slope.astype(F32)).astype(BF16)
+        dact = dot_nt(repeat(dmsg) * rows, weight)
+        dpre = dact.astype(BF16) * slope
         both = dot_nt(w_back[layer], dpre)
         return both[:basis] + both[basis:]
 
     def back_two(c, carry):
-        drad[c] = back(dmsg_two, rows_two[c], fout_two, ds_two[c], 1)
+        drad[c] = back(dmsg_two_low, rows_two[c], fout_two, ds_two[c], 1)
         return carry
 
+    dmsg_two_low = dmsg_two.astype(BF16)
     lax.fori_loop(0, chunks, back_two, 0, unroll=4)
     for copy in grad_copies:
         copy.wait_recv()
     dhidden = grad_all[0:atoms, :] + dot(sel_t[0], grad_in[0]) + dot(sel_t[1], grad_in[1])
     dupd_one = (dhidden * slope_one).astype(BF16)
-    dmsg_one = dot_nt(dupd_one, uw_ref[0])
+    dmsg_one = dot_nt(dupd_one, uw_ref[0]).astype(BF16)
 
     def back_one(c, carry):
         own, scattered = carry
@@ -352,7 +353,7 @@
 
     own, scattered = lax.fori_loop(
         0, chunks, back_one, (jnp.zeros((8, atoms), F32), jnp.zeros((16, ext), F32)),
-        unroll=4,
+        unroll=2,
     )
     scattered = scattered[0:8] + scattered[8:16]
     force_src[0] = scattered[:, atoms : 2 * atoms]
@@ -374,7 +375,7 @@
     tangent_row = rows_sum(tangent * tangent)
     speed = place([vel_ref[r] for r in range(3)])
     speed_row = rows_sum(speed * speed)
-    spring_part = spring_ref[0] * (ahead_norm - behind_norm)
+    spring_part = spring_ref[...] * (ahead_norm - behind_norm)
     local_force = own - scattered[:, 0:atoms]
     for copy in force_copies:
         copy.wait_recv()
@@ -403,7 +404,7 @@
     scale = 1.0 / jnp.sqrt(tangent_sq + EPSILON)
     parallel = along * scale
     unit_sq = tangent_sq * scale * scale
-    climbing = climb_ref[0] > 0
+    climbing = climb_ref[...] > 0
     take = jnp.where(climbing, 2.0 * parallel, parallel - spring_part)
     movable = jnp.where((image > 0) & (image < n_image - 1), 1.0, 0.0)
     band_sq = jnp.maximum(force_sq - 2.0 * take * parallel + take * take * unit_sq, 0.0)
@@ -416,10 +417,10 @@
         totals = totals + band_in[i]
     totals = jnp.sqrt(totals + EPSILON)
     force_norm, speed_norm = totals[0:1], totals[1:2]
-    mixing = mix_ref[0]
-    time_step = step_ref[0]
+    mixing = mix_ref[...]
+    time_step = step_ref[...]
     mixed = (1.0 - mixing) * speed + mixing * (speed_norm / force_norm) * band_force
-    kept = jnp.where(reset_ref[0] > 0, 0.0, mixed)
+    kept = jnp.where(reset_ref[...] > 0, 0.0, mixed)
     new_speed = (kept + time_step * band_force) * movable
     new_place = here + time_step * new_speed
     for r in range(3):
@@ -439,7 +440,7 @@
     atoms, per_atom = neighbours.shape
     channels = embed.shape[1]
     basis = filter_in.shape[1]
-    per_chunk = 2
+    per_chunk = 4
     chunks, pairs = per_atom // per_chunk, per_chunk * atoms
     ext = 3 * atoms
     vmem = pl.BlockSpec(memory_space=pltpu.VMEM)
@@ -453,15 +454,15 @@
         pltpu.VMEM((per_atom, atoms), jnp.int32),
         pltpu.VMEM((1, atoms), jnp.int32),
         pltpu.VMEM((1, atoms), jnp.int32),
-        pltpu.SMEM((1,), jnp.int32),
-        pltpu.SMEM((1,), jnp.int32),
+        pltpu.VMEM((1, 1), jnp.int32),
+        pltpu.VMEM((1, 1), jnp.int32),
         pltpu.VMEM(basis_shape, F32),
         pltpu.VMEM((2, channels, channels), BF16),
         pltpu.VMEM((2, channels, channels), BF16),
         pltpu.VMEM((1, channels), F32),
-        pltpu.SMEM((1,), F32),
-        pltpu.SMEM((1,), F32),
-        pltpu.SMEM((1,), F32),
+        pltpu.VMEM((1, 1), F32),
+        pltpu.VMEM((1, 1), F32),
+        pltpu.VMEM((1, 1), F32),
         dma((15,)),
         pltpu.VMEM((8, atoms), F32),
         pltpu.VMEM((8, atoms), F32),
@@ -518,9 +519,9 @@
         ),
     )(
         jnp.transpose(positions, (1, 0, 2)), jnp.transpose(velocity, (1, 0, 2)), embed,
-        neighbours.T, send_up.reshape(1, -1), send_down.reshape(1, -1), climb, reset,
+        neighbours.T, send_up.reshape(1, -1), send_down.reshape(1, -1), climb.reshape(1, 1), reset.reshape(1, 1),
         filter_in, filter_out, update_weight, readout.reshape(1, -1),
-        spring.reshape(1), time_step.reshape(1), mixing.reshape(1),
+        spring.reshape(1, 1), time_step.reshape(1, 1), mixing.reshape(1, 1),
     )
     back = (1, 0, 2)
     return jnp.transpose(new_pos, back), jnp.transpose(new_vel, back), energy.reshape(1)

time: 54.6 us -> 50.4 us (0.923)
  Pallas kernels: 46.9 us -> 42.6 us
    pallas_call x1, Pallas kernels: 46.9 us -> 42.6 us  [per_device(): pl.pallas_call(functools.partial(body, n_space, n_image), out_shape=(jax....]
where the time goes in v4:
time: 50.4 us; the launch traced here: 50.2 us
  Pallas kernels  42.6 us (85%)
  between operations  5.7 us (11%)
  local copies, waits for them, and re-layouts  1.85 us (4%)
    pallas_call x1, Pallas kernels, per_device(): pl.pallas_call(functools.partial(body, n_space, n_image), out_shape=(jax....  42.6 us
    unnamed x6, local copies, waits for them, and re-layouts  1.85 us

profile of v4, /device:TPU:0, one launch (start us, length us, event | category | flops | bytes accessed | tf_op | source)
XLA Modules:
  0.0 50.2 jit_solution(16169814391211068792)
XLA Ops:
  3.9 42.6 %shard_map.166 = (f32[3,1,128]{2,1,0:T(1,128)}, f32[3,1,128]{2,1,0:T(1,128)}, f32[1,1]{1,0:T(1,128)}) custom-call(f32[3,1,128]{2,1,0:T(1,128)} %bitcast.20, f32[3,1,128]{2,1,0:T(1,128)} %bitcast.21, bf16[128,128]{1,0:T(8,128)(2,1)} %emb_hbm.1, s32[32,128]{1,0:T(8,128)} %bitcast.19, s32[1,128]{1,0:T(1,128)} %bitcast.24, s32[1,128]{1,0:T(1,128)} %bitcast.25, ...), custom_call_target="tpu_custom_call" | custom-call | tf_op jit(solution)/shard_map/pallas_call | solution.py:507
  46.5 0.0 copy-start.1
  46.5 0.7 %copy-done.1 = f32[3,1,128]{2,1,0:T(1,128)S(1)} copy-done((f32[3,1,128]{2,1,0:T(1,128)S(1)}, f32[3,1,128]{2,1,0:T(1,128)}, u32[]{:S(2)}) %copy-start.1) | copy-done | bytes 1560
  47.1 0.0 copy-start
  47.1 0.6 %copy.26 = f32[1,3,128]{2,0,1:T(1,128)} copy(f32[1,3,128]{2,0,1:T(1,128)S(1)} %bitcast.23) | data formatting | bytes 3072
  47.7 0.1 copy-done
  47.8 0.6 %copy.27 = f32[1,3,128]{2,0,1:T(1,128)} copy(f32[1,3,128]{2,0,1:T(1,128)S(1)} %bitcast.22) | data formatting | bytes 3072
Async XLA Ops:
  46.5 0.7 %copy-start.1 = (f32[3,1,128]{2,1,0:T(1,128)S(1)}, f32[3,1,128]{2,1,0:T(1,128)}, u32[]{:S(2)}) copy-start(f32[3,1,128]{2,1,0:T(1,128)} %get-tuple-element.6) | copy-start | bytes 4612
  47.1 0.6 %copy-start = (f32[3,1,128]{2,1,0:T(1,128)S(1)}, f32[3,1,128]{2,1,0:T(1,128)}, u32[]{:S(2)}) copy-start(f32[3,1,128]{2,1,0:T(1,128)} %get-tuple-element.7) | copy-start | bytes 4612

commit v5 on v4

--- a/solution.py
+++ b/solution.py
@@ -279,7 +279,7 @@
         filt_two[c] = dot(act, fout_two)
         return carry
 
-    lax.fori_loop(0, chunks, filter_two, 0, unroll=4)
+    lax.fori_loop(0, chunks, filter_two, 0, unroll=2)
     for copy in hid_copies:
         copy.wait_recv()
     ext_hidden = ext_hid[...]
@@ -289,7 +289,7 @@
         rows_two[c] = rows.astype(BF16)
         return total + fold(filt_two[c] * rows)
 
-    msg_two = lax.fori_loop(0, chunks, layer_two, zeros, unroll=4)
+    msg_two = lax.fori_loop(0, chunks, layer_two, zeros, unroll=2)
     upd_two = dot(msg_two.astype(BF16), uw_ref[1])
     sig_two = gate(upd_two)
     act_two = upd_two * sig_two
@@ -333,7 +333,7 @@
         return carry
 
     dmsg_two_low = dmsg_two.astype(BF16)
-    lax.fori_loop(0, chunks, back_two, 0, unroll=4)
+    lax.fori_loop(0, chunks, back_two, 0, unroll=2)
     for copy in grad_copies:
         copy.wait_recv()
     dhidden = grad_all[0:atoms, :] + dot(sel_t[0], grad_in[0]) + dot(sel_t[1], grad_in[1])
@@ -440,7 +440,7 @@
     atoms, per_atom = neighbours.shape
     channels = embed.shape[1]
     basis = filter_in.shape[1]
-    per_chunk = 4
+    per_chunk = 8
     chunks, pairs = per_atom // per_chunk, per_chunk * atoms
     ext = 3 * atoms
     vmem = pl.BlockSpec(memory_space=pltpu.VMEM)

time: 50.4 us -> 47.1 us (0.935)
  Pallas kernels: 42.6 us -> 39.3 us
    pallas_call x1, Pallas kernels: 42.6 us -> 39.3 us  [per_device(): pl.pallas_call(functools.partial(body, n_space, n_image), out_shape=(jax....]
where the time goes in v5:
time: 47.1 us; the launch traced here: 46.9 us
  Pallas kernels  39.3 us (83%)
  between operations  5.7 us (12%)
  local copies, waits for them, and re-layouts  1.85 us (4%)
    pallas_call x1, Pallas kernels, per_device(): pl.pallas_call(functools.partial(body, n_space, n_image), out_shape=(jax....  39.3 us
    unnamed x6, local copies, waits for them, and re-layouts  1.85 us

profile of v5, /device:TPU:0, one launch (start us, length us, event | category | flops | bytes accessed | tf_op | source)
XLA Modules:
  0.0 46.9 jit_solution(11260277690497969716)
XLA Ops:
  3.9 39.3 %shard_map.166 = (f32[3,1,128]{2,1,0:T(1,128)}, f32[3,1,128]{2,1,0:T(1,128)}, f32[1,1]{1,0:T(1,128)}) custom-call(f32[3,1,128]{2,1,0:T(1,128)} %bitcast.20, f32[3,1,128]{2,1,0:T(1,128)} %bitcast.21, bf16[128,128]{1,0:T(8,128)(2,1)} %emb_hbm.1, s32[32,128]{1,0:T(8,128)} %bitcast.19, s32[1,128]{1,0:T(1,128)} %bitcast.24, s32[1,128]{1,0:T(1,128)} %bitcast.25, ...), custom_call_target="tpu_custom_call" | custom-call | tf_op jit(solution)/shard_map/pallas_call | solution.py:507
  43.2 0.0 copy-start.1
  43.2 0.7 %copy-done.1 = f32[3,1,128]{2,1,0:T(1,128)S(1)} copy-done((f32[3,1,128]{2,1,0:T(1,128)S(1)}, f32[3,1,128]{2,1,0:T(1,128)}, u32[]{:S(2)}) %copy-start.1) | copy-done | bytes 1560
  43.8 0.0 copy-start
  43.8 0.6 %copy.26 = f32[1,3,128]{2,0,1:T(1,128)} copy(f32[1,3,128]{2,0,1:T(1,128)S(1)} %bitcast.23) | data formatting | bytes 3072
  44.4 0.1 copy-done
  44.5 0.6 %copy.27 = f32[1,3,128]{2,0,1:T(1,128)} copy(f32[1,3,128]{2,0,1:T(1,128)S(1)} %bitcast.22) | data formatting | bytes 3072
Async XLA Ops:
  43.2 0.7 %copy-start.1 = (f32[3,1,128]{2,1,0:T(1,128)S(1)}, f32[3,1,128]{2,1,0:T(1,128)}, u32[]{:S(2)}) copy-start(f32[3,1,128]{2,1,0:T(1,128)} %get-tuple-element.6) | copy-start | bytes 4612
  43.8 0.6 %copy-start = (f32[3,1,128]{2,1,0:T(1,128)S(1)}, f32[3,1,128]{2,1,0:T(1,128)}, u32[]{:S(2)}) copy-start(f32[3,1,128]{2,1,0:T(1,128)} %get-tuple-element.7) | copy-start | bytes 4612

commit v6 on v5

--- a/solution.py
+++ b/solution.py
@@ -440,7 +440,7 @@
     atoms, per_atom = neighbours.shape
     channels = embed.shape[1]
     basis = filter_in.shape[1]
-    per_chunk = 8
+    per_chunk = 16
     chunks, pairs = per_atom // per_chunk, per_chunk * atoms
     ext = 3 * atoms
     vmem = pl.BlockSpec(memory_space=pltpu.VMEM)

time: 47.1 us -> 46 us (0.977)
  Pallas kernels: 39.3 us -> 38.2 us
    pallas_call x1, Pallas kernels: 39.3 us -> 38.2 us  [per_device(): pl.pallas_call(functools.partial(body, n_space, n_image), out_shape=(jax....]
where the time goes in v6:
time: 46 us; the launch traced here: 45.7 us
  Pallas kernels  38.2 us (83%)
  between operations  5.7 us (12%)
  local copies, waits for them, and re-layouts  1.85 us (4%)
    pallas_call x1, Pallas kernels, per_device(): pl.pallas_call(functools.partial(body, n_space, n_image), out_shape=(jax....  38.2 us
    unnamed x6, local copies, waits for them, and re-layouts  1.85 us

profile of v6, /device:TPU:0, one launch (start us, length us, event | category | flops | bytes accessed | tf_op | source)
XLA Modules:
  0.0 45.7 jit_solution(14501204226261378530)
XLA Ops:
  3.9 38.2 %shard_map.166 = (f32[3,1,128]{2,1,0:T(1,128)}, f32[3,1,128]{2,1,0:T(1,128)}, f32[1,1]{1,0:T(1,128)}) custom-call(f32[3,1,128]{2,1,0:T(1,128)} %bitcast.20, f32[3,1,128]{2,1,0:T(1,128)} %bitcast.21, bf16[128,128]{1,0:T(8,128)(2,1)} %emb_hbm.1, s32[32,128]{1,0:T(8,128)} %bitcast.19, s32[1,128]{1,0:T(1,128)} %bitcast.24, s32[1,128]{1,0:T(1,128)} %bitcast.25, ...), custom_call_target="tpu_custom_call" | custom-call | tf_op jit(solution)/shard_map/pallas_call | solution.py:507
  42.1 0.0 copy-start.1
  42.1 0.7 %copy-done.1 = f32[3,1,128]{2,1,0:T(1,128)S(1)} copy-done((f32[3,1,128]{2,1,0:T(1,128)S(1)}, f32[3,1,128]{2,1,0:T(1,128)}, u32[]{:S(2)}) %copy-start.1) | copy-done | bytes 1560
  42.7 0.0 copy-start
  42.7 0.6 %copy.26 = f32[1,3,128]{2,0,1:T(1,128)} copy(f32[1,3,128]{2,0,1:T(1,128)S(1)} %bitcast.23) | data formatting | bytes 3072
  43.3 0.1 copy-done
  43.4 0.6 %copy.27 = f32[1,3,128]{2,0,1:T(1,128)} copy(f32[1,3,128]{2,0,1:T(1,128)S(1)} %bitcast.22) | data formatting | bytes 3072
Async XLA Ops:
  42.1 0.7 %copy-start.1 = (f32[3,1,128]{2,1,0:T(1,128)S(1)}, f32[3,1,128]{2,1,0:T(1,128)}, u32[]{:S(2)}) copy-start(f32[3,1,128]{2,1,0:T(1,128)} %get-tuple-element.6) | copy-start | bytes 4612
  42.7 0.6 %copy-start = (f32[3,1,128]{2,1,0:T(1,128)S(1)}, f32[3,1,128]{2,1,0:T(1,128)}, u32[]{:S(2)}) copy-start(f32[3,1,128]{2,1,0:T(1,128)} %get-tuple-element.7) | copy-start | bytes 4612
